TPU v7x, 512 devices: a whole 4x8x8 slice. The times are simulated.
512 devices in a mesh: frame: 32 (over z, x), feat: 16 (over y, core).
Axes of the slice: x: 4, y: 8, z: 8, core: 2. Of those that a mesh axis runs over, the one named last changes fastest.
Arguments:
- trajectory: bfloat16 [24576, 24576], P('frame', 'feat'), may hold values from -40 to 40
- test_matrix: bfloat16 [24576, 512], P('feat'), may hold values from -0.0390625 to 0.0390625
Outputs:
- orthobasis: bfloat16 [24576, 512], P('frame')
- projected: bfloat16 [512, 24576], P('frame', 'feat')
- small_gram: float32 [512, 512], P('frame')
All inputs are finite; a program needn't handle non-finite values.
Results may differ from a plain program's by a relative error of at most 0.015.
Values may be sent and summed in bfloat16 or wider, within the bound.
No kernel may reach another device: no remote copies, remote signals or barrier semaphores. Data moves between devices by JAX's collectives and lax.ppermute only.
A program may use at most 64 MiB of HBM per device.

v0:
```python
import math

import jax
import jax.numpy as jnp
from jax import lax
from jax.sharding import PartitionSpec as P


def gram_part(sketch, frames_all):
    return jnp.dot(sketch.T, sketch, precision=lax.Precision.HIGHEST) / frames_all


def to_basis(sketch, gram):
    factor = jnp.linalg.cholesky(gram)
    solved = jax.scipy.linalg.solve_triangular(factor, sketch.T, lower=True)
    return solved.T.astype(jnp.bfloat16)


def per_device(trajectory, test_matrix):
    frame_count = lax.axis_size("frame")
    feat_count = lax.axis_size("feat")
    local_rows = trajectory.shape[0]
    frames_all = local_rows * frame_count
    features_all = trajectory.shape[1] * feat_count
    partial_sketch = jnp.dot(trajectory, test_matrix, preferred_element_type=jnp.float32)
    sketch = lax.psum(partial_sketch, "feat")
    gram = lax.psum(gram_part(sketch, frames_all), "frame")
    orthobasis = to_basis(sketch, gram)
    summed = lax.psum_scatter(
        lax.dot_general(
            orthobasis, trajectory, (((0,), (0,)), ((), ())), preferred_element_type=jnp.float32
        ),
        "frame",
        scatter_dimension=0,
        tiled=True,
    )
    projected = (summed / math.sqrt(frames_all)).astype(jnp.bfloat16)
    partial_gram = (
        lax.dot_general(
            projected,
            lax.all_gather(projected, "frame", axis=0, tiled=True),
            (((1,), (1,)), ((), ())),
            preferred_element_type=jnp.float32,
        )
        / features_all
    )
    small_gram = lax.psum(partial_gram.astype(jnp.bfloat16), "feat").astype(jnp.float32)
    return (orthobasis, projected, small_gram)


def solution(mesh):
    return jax.shard_map(
        per_device,
        mesh=mesh,
        in_specs=(P("frame", "feat"), P("feat", None)),
        out_specs=(P("frame", None), P("frame", "feat"), P("frame", None)),
        check_vma=False,
    )
```

profile of v0, /device:TPU:1, one launch (start us, length us, event | category | flops | bytes accessed | tf_op | source)
XLA Modules:
  0.0 831.8 jit_solution(5573328998534356638)
XLA Ops:
  7.2 1.6 copy-done
  8.8 3.9 fusion.37
  12.8 123.8 %all-reduce.4.cloned.1.call-done = f32[768,512]{1,0:T(8,128)} async-done(((f32[768,512]{1,0:T(8,128)}), f32[768,512]{1,0:T(8,128)}) %all-reduce.4.cloned.1.call-update) | async-done | bytes 1572880 | tf_op jit(solution)/shard_map/psum | solution.py:26
  136.7 5.6 convolution_multiply_fusion
  142.8 156.8 %all-reduce.6.cloned.1.call-done = f32[512,512]{0,1:T(8,128)} async-done(((f32[512,512]{0,1:T(8,128)}), f32[512,512]{0,1:T(8,128)}) %all-reduce.6.cloned.1.call-update) | async-done | bytes 1048592 | tf_op jit(solution)/shard_map/psum | solution.py:27
  299.6 2.6 copy.6
  302.3 1.4 fusion.6
  304.7 11.7 %cholesky.104 = f32[128,128]{1,0:T(8,128)S(1)} custom-call(f32[128,128]{1,0:T(8,128)S(1)} %cholesky.266), custom_call_target="Cholesky" | custom-call | tf_op jit(solution)/shard_map/jit(cholesky)/cholesky | solution.py:14
  316.4 9.8 %custom-call.31 = f32[1,128,128]{1,2,0:T(8,128)S(1)} custom-call(f32[1,128,128]{2,1,0:T(8,128)S(1)} %get-tuple-element.33), custom_call_target="InvertDiagBlocksLowerTriangular" | custom-call | tf_op jit(solution)/shard_map/jit(cholesky)/cholesky | solution.py:14
  329.6 11.7 %cholesky.217 = f32[128,128]{1,0:T(8,128)S(1)} custom-call(f32[128,128]{1,0:T(8,128)S(1)} %cholesky.270), custom_call_target="Cholesky" | custom-call | tf_op jit(solution)/shard_map/jit(cholesky)/cholesky | solution.py:14
  341.3 9.9 %custom-call.32 = f32[1,128,128]{1,2,0:T(8,128)S(1)} custom-call(f32[1,128,128]{2,1,0:T(8,128)S(1)} %get-tuple-element.30), custom_call_target="InvertDiagBlocksLowerTriangular" | custom-call | tf_op jit(solution)/shard_map/jit(cholesky)/cholesky | solution.py:14
  354.4 13.2 %cholesky.238 = f32[128,128]{1,0:T(8,128)} custom-call(f32[128,128]{1,0:T(8,128)} %cholesky.275), custom_call_target="Cholesky" | custom-call | tf_op jit(solution)/shard_map/jit(cholesky)/cholesky | solution.py:14
  367.5 1.5 select_reduce_fusion.1
  369.7 11.3 %custom-call.33 = f32[1,128,128]{1,2,0:T(8,128)} custom-call(f32[1,128,128]{2,1,0:T(8,128)} %get-tuple-element.27), custom_call_target="InvertDiagBlocksLowerTriangular" | custom-call | tf_op jit(solution)/shard_map/jit(cholesky)/cholesky | solution.py:14
  383.2 11.7 %cholesky.255 = f32[128,128]{1,0:T(8,128)S(1)} custom-call(f32[128,128]{1,0:T(8,128)S(1)} %convolution_subtract_fusion.5), custom_call_target="Cholesky" | custom-call | tf_op jit(solution)/shard_map/jit(cholesky)/cholesky | solution.py:14
  398.9 1.3 select_select_fusion
  400.2 13.9 %while.1 = (s32[]{:T(128)}, f32[512,512]{1,0:T(8,128)}, s32[4,2]{0,1:T(2,128)S(1)}, f32[4,128,128]{2,1,0:T(8,128)}, s32[]{:T(128)}) while((s32[]{:T(128)}, f32[512,512]{1,0:T(8,128)}, s32[4,2]{0,1:T(2,128)S(1)}, f32[4,128,128]{2,1,0:T(8,128)}, s32[]{:T(128)}) %tuple.35), condition=%wide.while_cond, body=%wide.while_body.sunk | while | flops 2 | bytes 132705 | solution.py:15
  400.8 2.9 bitcast_dynamic-update-slice_fusion.2
  404.3 2.9 bitcast_dynamic-update-slice_fusion.2
  407.8 2.9 bitcast_dynamic-update-slice_fusion.2
  411.3 2.8 bitcast_dynamic-update-slice_fusion.2
  414.1 40.1 %custom-call.34 = f32[4,128,128]{1,2,0:T(8,128)S(1)} custom-call(f32[4,128,128]{2,1,0:T(8,128)} %get-tuple-element.10), custom_call_target="InvertDiagBlocksLowerTriangular" | custom-call | tf_op jit(solution)/shard_map/jit(_solve_triangular)/triangular_solve | solution.py:15
  454.3 1.6 fusion.36
  455.9 1.8 convolution_subtract_fusion.1
  458.3 2.3 convolution_subtract_fusion.2
  461.2 3.1 convolution_subtract_fusion
  465.4 3.1 fusion.17
  468.5 221.0 %reduce-scatter.2.cloned.1.call-done = f32[16,1536]{1,0:T(8,128)} async-done(((f32[512,1536]{1,0:T(8,128)}), f32[16,1536]{1,0:T(8,128)}) %reduce-scatter.2.cloned.1.call-update) | async-done | bytes 98320 | tf_op jit(solution)/shard_map/reduce_scatter | solution.py:29
  689.5 1.5 multiply_convert_fusion
  693.3 82.4 %all-gather.2.cloned.1.call-done = bf16[512,1536]{1,0:T(8,128)(2,1)} async-done(((bf16[16,1536]{1,0:T(8,128)(2,1)}), bf16[512,1536]{1,0:T(8,128)(2,1)}) %all-gather.2.cloned.1.call-update) | async-done | bytes 1572880 | tf_op jit(solution)/shard_map/all_gather | solution.py:41
  775.7 1.9 fusion.5
  777.6 46.8 %psum.23 = bf16[16,512]{1,0:T(8,128)(2,1)S(1)} all-reduce(bf16[16,512]{1,0:T(8,128)(2,1)S(1)} %fusion.5), channel_id=1, replica_groups=mesh['frame'=32,'feat'=16] {'feat'}, use_global_device_ids=true, to_apply=%region_11.12 | all-reduce | flops 8192 | bytes 32768 | tf_op jit(solution)/shard_map/psum | solution.py:47
  (56 shorter events, 19.9 us)
Async XLA Ops:
  7.2 1.7 copy-start
  7.2 129.5 %all-reduce.4.cloned.1.call-start = ((), (), s32[]{:S(2)}) async-start(), calls=%async_computation.1 | async-start | bytes 3145728 | tf_op jit(solution)/shard_map/psum | solution.py:26
  12.8 286.8 %all-reduce.6.cloned.1.call-start = ((), (), s32[]{:S(2)}) async-start(), calls=%async_computation.2 | async-start | bytes 2097152 | tf_op jit(solution)/shard_map/psum | solution.py:27
  142.3 547.2 %reduce-scatter.2.cloned.1.call-start = ((), (), s32[]{:S(2)}) async-start(), calls=%async_computation.3 | async-start | bytes 3244032 | tf_op jit(solution)/shard_map/reduce_scatter | solution.py:29
  299.6 2.6 copy-start.2
  303.7 1.0 copy-start.3
  328.9 0.7 copy-start.6
  454.3 4.0 copy-start.1
  461.1 3.6 copy-start.4
  464.7 0.7 copy-start.5
  468.5 307.2 %all-gather.2.cloned.1.call-start = ((), (), s32[]{:S(2)}) async-start(), calls=%async_computation.4 | async-start | bytes 1622016 | tf_op jit(solution)/shard_map/all_gather | solution.py:41
  692.1 83.5 %copy-start.7 = (bf16[16,1536]{1,0:T(8,128)(2,1)S(1)}, bf16[16,1536]{1,0:T(8,128)(2,1)}, u32[]{:S(2)}) copy-start(bf16[16,1536]{1,0:T(8,128)(2,1)} %multiply_convert_fusion) | copy-start | bytes 147460
Sparse Core Ops, SparseCore 0:
  12.9 123.7 all-reduce.3
  142.4 157.1 all-reduce.5
  468.6 220.8 reduce-scatter.1
  693.1 82.5 all-gather.1
where the time goes:
time: 838 us; the launch traced here: 832 us
  waiting for transfers between devices  584 us (70%)
  other arithmetic  129 us (15%)
  blocking collectives  46.8 us (6%)
  matrix products  32.1 us (4%)
  local copies, waits for them, and re-layouts  22.4 us (3%)
  between operations  16.8 us (2%)
    reduce_scatter x1, waiting for transfers between devices, per_device(): lax.psum_scatter(lax.dot_general(orthobasis, trajectory, (((0,), (0,)), (...  221 us
    psum x1, waiting for transfers between devices, per_device(): gram = lax.psum(gram_part(sketch, frames_all), 'frame')  157 us
    psum x1, waiting for transfers between devices, per_device(): sketch = lax.psum(partial_sketch, 'feat')  124 us
    another operation x14, other arithmetic, to_basis(): factor = jnp.linalg.cholesky(gram)  83 us
    all_gather x1, waiting for transfers between devices, per_device(): lax.all_gather(projected, 'frame', axis=0, tiled=True)  82.4 us
    psum x1, blocking collectives, per_device(): lax.psum(partial_gram.astype(jnp.bfloat16), 'feat').astype(jnp.float32)  46.8 us
    another operation x3, other arithmetic, to_basis(): solved = jax.scipy.linalg.solve_triangular(factor, sketch.T, lower=True)  41.4 us
  transfers between devices with their start and end apart: 4, of which 4 were waited for; matrix products, arithmetic and copies ran while one was open for 0% of the time, Pallas kernels for 0%

commit v1 on v0

v1 whole, which is shorter than its diff:
```python
import math

import jax
import jax.numpy as jnp
from jax import lax
from jax.sharding import PartitionSpec as P


def lines(axis_size, stride):
    return [list(range(s, axis_size, stride)) for s in range(stride)]


def scatter_sum(blocks, axis, groups=None):
    got = lax.all_to_all(blocks, axis, 0, 0, axis_index_groups=groups)
    return jnp.sum(got.astype(jnp.float32), axis=0)


def gather(block, axis, count, groups=None):
    copies = jnp.broadcast_to(block, (count,) + block.shape)
    return lax.all_to_all(copies, axis, 0, 0, axis_index_groups=groups)


def swap_cores(block):
    count = lax.axis_size("feat")
    return lax.ppermute(block, "feat", [(i, i ^ 1) for i in range(count)])


def feat_scatter_sum(whole):
    count = lax.axis_size("feat")
    core = lax.axis_index("feat") % 2
    rows, columns = whole.shape
    halves = whole.reshape(2, rows // 2, columns)
    keep = lax.dynamic_index_in_dim(halves, core, 0, keepdims=False)
    give = lax.dynamic_index_in_dim(halves, 1 - core, 0, keepdims=False)
    half = keep + swap_cores(give)
    return scatter_sum(half.reshape(count // 2, -1, columns), "feat", lines(count, 2))


def feat_gather(block):
    count = lax.axis_size("feat")
    core = lax.axis_index("feat") % 2
    half = gather(block, "feat", count // 2, lines(count, 2)).reshape(-1, block.shape[1])
    other = swap_cores(half)
    low = jnp.where(core == 0, half, other)
    high = jnp.where(core == 0, other, half)
    return jnp.concatenate([low, high], axis=0)


def to_basis(sketch, gram):
    factor = jnp.linalg.cholesky(gram)
    solved = jax.scipy.linalg.solve_triangular(factor, sketch.T, lower=True)
    return solved.T.astype(jnp.bfloat16)


def per_device(trajectory, test_matrix):
    frame_count = lax.axis_size("frame")
    feat_count = lax.axis_size("feat")
    local_rows, local_feats = trajectory.shape
    frames_all = local_rows * frame_count
    features_all = local_feats * feat_count
    rank = test_matrix.shape[1]

    partial_sketch = jnp.dot(trajectory, test_matrix, preferred_element_type=jnp.float32)
    sketch = feat_gather(feat_scatter_sum(partial_sketch))

    width = rank // feat_count
    place = lax.axis_index("feat") % 2 * (feat_count // 2) + lax.axis_index("feat") // 2
    columns = lax.dynamic_slice_in_dim(sketch, place * width, width, axis=1)
    gram_rows = jnp.dot(columns.T, sketch, precision=lax.Precision.HIGHEST) / frames_all
    gram_mine = scatter_sum(gram_rows.reshape(frame_count, -1, rank), "frame")
    gram_rows = gather(gram_mine, "frame", frame_count).reshape(width, rank)
    gram = feat_gather(gram_rows)

    orthobasis = to_basis(sketch, gram)
    partial = lax.dot_general(
        trajectory, orthobasis, (((0,), (0,)), ((), ())), preferred_element_type=jnp.float32
    )
    summed = scatter_sum(partial.astype(jnp.bfloat16).reshape(frame_count, -1, rank), "frame")
    features_mine = (summed / math.sqrt(frames_all)).astype(jnp.bfloat16)

    by_rows = features_mine.T.reshape(frame_count, rank // frame_count, -1)
    swapped = lax.all_to_all(by_rows, "frame", 0, 0)
    projected = swapped.transpose(1, 0, 2).reshape(rank // frame_count, local_feats)

    partial_gram = lax.dot_general(
        features_mine, features_mine, (((0,), (0,)), ((), ())), preferred_element_type=jnp.float32
    )
    gram_mine = scatter_sum(
        partial_gram.astype(jnp.bfloat16).reshape(frame_count, -1, rank), "frame"
    )
    small_gram = jnp.sum(gather(gram_mine, "feat", feat_count), axis=0) / features_all
    return (orthobasis, projected, small_gram)


def solution(mesh):
    return jax.shard_map(
        per_device,
        mesh=mesh,
        in_specs=(P("frame", "feat"), P("feat", None)),
        out_specs=(P("frame", None), P("frame", "feat"), P("frame", None)),
        check_vma=False,
    )
```

time: 838 us -> 423 us (0.50)
  waiting for transfers between devices: 584 us -> 41.5 us
  blocking collectives: 46.8 us -> 144 us
  starting transfers between devices: 0.63 us -> 36.1 us
  between operations: 16.8 us -> 4 us
  local copies, waits for them, and re-layouts: 22.4 us -> 32.7 us
  matrix products: 32.1 us -> 23.1 us
    psum x2 -> x0, waiting for transfers between devices: 281 us -> none  [the longest x1 157 us: per_device(): gram = lax.psum(gram_part(sketch, frames_all), 'frame')]
    reduce_scatter x1 -> x0, waiting for transfers between devices: 221 us -> none  [per_device(): lax.psum_scatter(lax.dot_general(orthobasis, trajectory, (((0,), (0,)), (...]
    all_to_all x0 -> x6, blocking collectives: none -> 144 us  [the longest x3 88.7 us: scatter_sum(): got = lax.all_to_all(blocks, axis, 0, 0, axis_index_groups=groups)]
    all_gather x1 -> x0, waiting for transfers between devices: 82.4 us -> none  [per_device(): lax.all_gather(projected, 'frame', axis=0, tiled=True)]
    psum x1 -> x0, blocking collectives: 46.8 us -> none  [per_device(): lax.psum(partial_gram.astype(jnp.bfloat16), 'feat').astype(jnp.float32)]
    all_to_all x0 -> x3, waiting for transfers between devices: none -> 37.2 us  [the longest x1 14.3 us: scatter_sum(): got = lax.all_to_all(blocks, axis, 0, 0, axis_index_groups=groups)]
    ppermute x0 -> x3, starting transfers between devices: none -> 18.2 us  [swap_cores(): return lax.ppermute(block, 'feat', [(i, i ^ 1) for i in range(count)])]
    all_to_all x0 -> x3, starting transfers between devices: none -> 17.9 us  [the longest x1 7.01 us: gather(): return lax.all_to_all(copies, axis, 0, 0, axis_index_groups=groups)]
  transfers between devices with their start and end apart: 4 -> 6, of which waited for: 4 -> 5; matrix products, arithmetic and copies ran while one was open for 0% -> 2% of each run, Pallas kernels for 0% -> 0%
where the time goes in v1:
time: 423 us; the launch traced here: 417 us
  blocking collectives  144 us (34%)
  other arithmetic  136 us (32%)
  waiting for transfers between devices  41.5 us (10%)
  starting transfers between devices  36.1 us (9%)
  local copies, waits for them, and re-layouts  32.7 us (8%)
  matrix products  23.1 us (5%)
    all_to_all x3, blocking collectives, scatter_sum(): got = lax.all_to_all(blocks, axis, 0, 0, axis_index_groups=groups)  88.7 us
    another operation x14, other arithmetic, to_basis(): factor = jnp.linalg.cholesky(gram)  83.2 us
    all_to_all x3, blocking collectives, gather(): return lax.all_to_all(copies, axis, 0, 0, axis_index_groups=groups)  54.8 us
    another operation x3, other arithmetic, to_basis(): solved = jax.scipy.linalg.solve_triangular(factor, sketch.T, lower=True)  41.2 us
    ppermute x3, starting transfers between devices, swap_cores(): return lax.ppermute(block, 'feat', [(i, i ^ 1) for i in range(count)])  18.2 us
    all_to_all x1, waiting for transfers between devices, scatter_sum(): got = lax.all_to_all(blocks, axis, 0, 0, axis_index_groups=groups)  14.3 us
    all_to_all x1, waiting for transfers between devices, gather(): return lax.all_to_all(copies, axis, 0, 0, axis_index_groups=groups)  14.2 us
    another operation x12, local copies, waits for them, and re-layouts  14 us
  transfers between devices with their start and end apart: 6, of which 5 were waited for; matrix products, arithmetic and copies ran while one was open for 2% of the time, Pallas kernels for 0%

profile of v1, /device:TPU:1, one launch (start us, length us, event | category | flops | bytes accessed | tf_op | source)
XLA Modules:
  0.0 417.4 jit_solution(15551937149850535700)
XLA Ops:
  2.3 2.8 fusion.49
  7.2 8.8 %collective-permute-start = (f32[384,512]{1,0:T(8,128)}, f32[384,512]{1,0:T(8,128)S(1)}, u32[]{:S(2)}, u32[]{:S(2)}) collective-permute-start(f32[384,512]{1,0:T(8,128)} %dynamic-slice_bitcast_fusion), channel_id=1, source_target_pairs={{0,1},{1,0},{2,3},{3,2},{4,5},{5,4},{6,7},{7,6},{8,9},{9,8},{10,11... | collective-permute-start | bytes 2359304 | tf_op jit(solution)/shard_map/ppermute | solution.py:25
  19.3 26.0 %all_to_all.45 = f32[8,48,512]{2,1,0:T(8,128)S(1)} all-to-all(f32[8,48,512]{2,1,0:T(8,128)S(1)} %bitcast.80), channel_id=1, replica_groups={{0,2,4,6,8,10,12,14},{1,3,5,7,9,11,13,15},{16,18,20,22,24,26,28,30},{17..., dimensions={0} | all-to-all | bytes 1572864 | tf_op jit(solution)/shard_map/all_to_all | solution.py:14
  45.5 25.9 %all_to_all.46 = f32[8,48,512]{2,1,0:T(8,128)S(1)} all-to-all(f32[8,48,512]{2,1,0:T(8,128)S(1)} %broadcast_in_dim.14), channel_id=1, replica_groups={{0,2,4,6,8,10,12,14},{1,3,5,7,9,11,13,15},{16,18,20,22,24,26,28,30},{17..., dimensions={0} | all-to-all | bytes 1572864 | tf_op jit(solution)/shard_map/all_to_all | solution.py:20
  72.5 2.5 collective-permute-start.1
  80.4 19.1 %all_to_all.47 = f32[32,1,512]{2,1,0:T(1,128)S(1)} all-to-all(f32[32,1,512]{2,1,0:T(1,128)S(1)} %copy.45), channel_id=1, replica_groups=mesh['frame'=32,'feat'=16] {'frame'}, dimensions={0} | all-to-all | bytes 131072 | tf_op jit(solution)/shard_map/all_to_all | solution.py:14
  99.6 11.9 %all_to_all.48 = f32[32,1,512]{2,1,0:T(1,128)S(1)} all-to-all(f32[32,1,512]{2,1,0:T(1,128)S(1)} %broadcast_in_dim.15), channel_id=1, replica_groups=mesh['frame'=32,'feat'=16] {'frame'}, dimensions={0} | all-to-all | bytes 131072 | tf_op jit(solution)/shard_map/all_to_all | solution.py:20
  111.6 17.0 %all_to_all.49 = f32[8,32,512]{2,1,0:T(8,128)} all-to-all(f32[8,32,512]{2,1,0:T(8,128)S(1)} %broadcast_in_dim.16), channel_id=1, replica_groups={{0,2,4,6,8,10,12,14},{1,3,5,7,9,11,13,15},{16,18,20,22,24,26,28,30},{17..., dimensions={0} | all-to-all | bytes 1048576 | tf_op jit(solution)/shard_map/all_to_all | solution.py:20
  130.6 6.9 %collective-permute-start.2 = (f32[256,512]{0,1:T(8,128)}, f32[256,512]{0,1:T(8,128)}, u32[]{:S(2)}, u32[]{:S(2)}) collective-permute-start(f32[256,512]{0,1:T(8,128)} %copy.47), channel_id=1, source_target_pairs={{0,1},{1,0},{2,3},{3,2},{4,5},{5,4},{6,7},{7,6},{8,9},{9,8},{10,11... | collective-permute-start | bytes 1572872 | tf_op jit(solution)/shard_map/ppermute | solution.py:25
  142.2 2.6 copy.49
  147.2 11.7 %cholesky.104 = f32[128,128]{1,0:T(8,128)S(1)} custom-call(f32[128,128]{1,0:T(8,128)S(1)} %cholesky.266), custom_call_target="Cholesky" | custom-call | tf_op jit(solution)/shard_map/jit(cholesky)/cholesky | solution.py:50
  159.0 9.8 %custom-call.31 = f32[1,128,128]{1,2,0:T(8,128)S(1)} custom-call(f32[1,128,128]{2,1,0:T(8,128)S(1)} %get-tuple-element.52), custom_call_target="InvertDiagBlocksLowerTriangular" | custom-call | tf_op jit(solution)/shard_map/jit(cholesky)/cholesky | solution.py:50
  172.1 11.7 %cholesky.217 = f32[128,128]{1,0:T(8,128)S(1)} custom-call(f32[128,128]{1,0:T(8,128)S(1)} %cholesky.270), custom_call_target="Cholesky" | custom-call | tf_op jit(solution)/shard_map/jit(cholesky)/cholesky | solution.py:50
  183.8 10.0 %custom-call.32 = f32[1,128,128]{1,2,0:T(8,128)S(1)} custom-call(f32[1,128,128]{2,1,0:T(8,128)S(1)} %get-tuple-element.49), custom_call_target="InvertDiagBlocksLowerTriangular" | custom-call | tf_op jit(solution)/shard_map/jit(cholesky)/cholesky | solution.py:50
  196.9 13.2 %cholesky.238 = f32[128,128]{1,0:T(8,128)} custom-call(f32[128,128]{1,0:T(8,128)} %cholesky.275), custom_call_target="Cholesky" | custom-call | tf_op jit(solution)/shard_map/jit(cholesky)/cholesky | solution.py:50
  212.2 11.3 %custom-call.33 = f32[1,128,128]{1,2,0:T(8,128)} custom-call(f32[1,128,128]{2,1,0:T(8,128)} %get-tuple-element.46), custom_call_target="InvertDiagBlocksLowerTriangular" | custom-call | tf_op jit(solution)/shard_map/jit(cholesky)/cholesky | solution.py:50
  225.8 11.9 %cholesky.255 = f32[128,128]{1,0:T(8,128)S(1)} custom-call(f32[128,128]{1,0:T(8,128)S(1)} %convolution_subtract_fusion.2), custom_call_target="Cholesky" | custom-call | tf_op jit(solution)/shard_map/jit(cholesky)/cholesky | solution.py:50
  242.8 14.0 %while.1 = (s32[]{:T(128)}, f32[512,512]{1,0:T(8,128)}, s32[4,2]{0,1:T(2,128)S(1)}, f32[4,128,128]{2,1,0:T(8,128)}, s32[]{:T(128)}) while((s32[]{:T(128)}, f32[512,512]{1,0:T(8,128)}, s32[4,2]{0,1:T(2,128)S(1)}, f32[4,128,128]{2,1,0:T(8,128)}, s32[]{:T(128)}) %tuple.42), condition=%wide.while_cond, body=%wide.while_body.sunk | while | flops 2 | bytes 132705 | solution.py:51
  243.4 2.9 bitcast_dynamic-update-slice_fusion.2
  246.9 2.9 bitcast_dynamic-update-slice_fusion.2
  250.4 2.9 bitcast_dynamic-update-slice_fusion.2
  254.0 2.8 bitcast_dynamic-update-slice_fusion.2
  256.8 40.1 %custom-call.34 = f32[4,128,128]{1,2,0:T(8,128)S(1)} custom-call(f32[4,128,128]{2,1,0:T(8,128)} %get-tuple-element.10), custom_call_target="InvertDiagBlocksLowerTriangular" | custom-call | tf_op jit(solution)/shard_map/jit(_solve_triangular)/triangular_solve | solution.py:51
  305.0 2.5 fusion
  307.6 2.6 copy.50
  310.1 43.7 %all_to_all.50 = bf16[32,48,512]{2,1,0:T(8,128)(2,1)S(1)} all-to-all(bf16[32,48,512]{2,1,0:T(8,128)(2,1)} %bitcast.79), channel_id=1, replica_groups=mesh['frame'=32,'feat'=16] {'frame'}, dimensions={0} | all-to-all | bytes 3145728 | tf_op jit(solution)/shard_map/all_to_all | solution.py:14
  355.2 4.8 %all-to-all-start.7 = ((bf16[32,16,512]{2,1,0:T(8,128)(2,1)}), bf16[32,16,512]{2,1,0:T(8,128)(2,1)S(1)}, u32[]{:S(2)}, u32[]{:S(2)}) async-start(bf16[32,16,512]{2,1,0:T(8,128)(2,1)} %bitcast.25), calls=%async_computation.7 | async-start | bytes 1048576 | tf_op jit(solution)/shard_map/all_to_all | solution.py:14
  360.9 14.3 %all-to-all-done.7 = bf16[32,16,512]{2,1,0:T(8,128)(2,1)S(1)} async-done(((bf16[32,16,512]{2,1,0:T(8,128)(2,1)}), bf16[32,16,512]{2,1,0:T(8,128)(2,1)S(1)}, u32[]{:S(2)}, u32[]{:S(2)}) %all-to-all-start.7) | async-done | bytes 524320 | tf_op jit(solution)/shard_map/all_to_all | solution.py:14
  375.2 6.2 %all-to-all-start.6 = ((bf16[32,2,384]{2,1,0:T(2,128)(2,1)}), bf16[32,2,384]{2,1,0:T(2,128)(2,1)S(1)}, u32[]{:S(2)}, u32[]{:S(2)}) async-start(bf16[32,2,384]{2,1,0:T(2,128)(2,1)} %reshape.107), calls=%async_computation.6 | async-start | bytes 98304 | tf_op jit(solution)/shard_map/all_to_all | solution.py:82
  381.5 8.6 %all-to-all-done.6 = bf16[32,2,384]{2,1,0:T(2,128)(2,1)S(1)} async-done(((bf16[32,2,384]{2,1,0:T(2,128)(2,1)}), bf16[32,2,384]{2,1,0:T(2,128)(2,1)S(1)}, u32[]{:S(2)}, u32[]{:S(2)}) %all-to-all-start.6) | async-done | bytes 49184 | tf_op jit(solution)/shard_map/all_to_all | solution.py:82
  391.0 7.0 %all-to-all-start.8 = ((f32[16,16,512]{2,1,0:T(8,128)}), f32[16,16,512]{2,1,0:T(8,128)}, u32[]{:S(2)}, u32[]{:S(2)}) async-start(f32[16,16,512]{2,1,0:T(8,128)} %broadcast_in_dim.17), calls=%async_computation.8 | async-start | bytes 1048576 | tf_op jit(solution)/shard_map/all_to_all | solution.py:20
  401.3 14.2 %all-to-all-done.8 = f32[16,16,512]{2,1,0:T(8,128)} async-done(((f32[16,16,512]{2,1,0:T(8,128)}), f32[16,16,512]{2,1,0:T(8,128)}, u32[]{:S(2)}, u32[]{:S(2)}) %all-to-all-start.8) | async-done | bytes 524320 | tf_op jit(solution)/shard_map/all_to_all | solution.py:20
  (92 shorter events, 54.9 us)
Async XLA Ops:
  0.6 1.7 copy-start
  5.1 1.2 copy-start.5
  7.2 10.9 %collective-permute-start = (f32[384,512]{1,0:T(8,128)}, f32[384,512]{1,0:T(8,128)S(1)}, u32[]{:S(2)}, u32[]{:S(2)}) collective-permute-start(f32[384,512]{1,0:T(8,128)} %dynamic-slice_bitcast_fusion), channel_id=1, source_target_pairs={{0,1},{1,0},{2,3},{3,2},{4,5},{5,4},{6,7},{7,6},{8,9},{9,8},{10,11... | collective-permute-start | bytes 2359304 | tf_op jit(solution)/shard_map/ppermute | solution.py:25
  72.5 4.7 %collective-permute-start.1 = (f32[384,512]{0,1:T(8,128)}, f32[384,512]{0,1:T(8,128)}, u32[]{:S(2)}, u32[]{:S(2)}) collective-permute-start(f32[384,512]{0,1:T(8,128)} %copy.43), channel_id=1, source_target_pairs={{0,1},{1,0},{2,3},{3,2},{4,5},{5,4},{6,7},{7,6},{8,9},{9,8},{10,11... | collective-permute-start | bytes 2359304 | tf_op jit(solution)/shard_map/ppermute | solution.py:25
  78.7 1.6 copy-start.1
  130.6 9.4 %collective-permute-start.2 = (f32[256,512]{0,1:T(8,128)}, f32[256,512]{0,1:T(8,128)}, u32[]{:S(2)}, u32[]{:S(2)}) collective-permute-start(f32[256,512]{0,1:T(8,128)} %copy.47), channel_id=1, source_target_pairs={{0,1},{1,0},{2,3},{3,2},{4,5},{5,4},{6,7},{7,6},{8,9},{9,8},{10,11... | collective-permute-start | bytes 1572872 | tf_op jit(solution)/shard_map/ppermute | solution.py:25
  137.5 2.5 copy-start.4
  146.2 1.0 copy-start.3
  171.4 0.7 copy-start.8
  296.9 3.0 copy-start.2
  300.5 4.5 %copy-start.6 = (bf16[128,768]{1,0:T(8,128)(2,1)}, bf16[128,768]{1,0:T(8,128)(2,1)S(1)}, u32[]{:S(2)}) copy-start(bf16[128,768]{1,0:T(8,128)(2,1)S(1)} %get-tuple-element.57) | copy-start | bytes 589828
  302.6 2.4 copy-start.7
  355.2 20.1 %all-to-all-start.7 = ((bf16[32,16,512]{2,1,0:T(8,128)(2,1)}), bf16[32,16,512]{2,1,0:T(8,128)(2,1)S(1)}, u32[]{:S(2)}, u32[]{:S(2)}) async-start(bf16[32,16,512]{2,1,0:T(8,128)(2,1)} %bitcast.25), calls=%async_computation.7 | async-start | bytes 1048576 | tf_op jit(solution)/shard_map/all_to_all | solution.py:14
  375.2 14.9 %all-to-all-start.6 = ((bf16[32,2,384]{2,1,0:T(2,128)(2,1)}), bf16[32,2,384]{2,1,0:T(2,128)(2,1)S(1)}, u32[]{:S(2)}, u32[]{:S(2)}) async-start(bf16[32,2,384]{2,1,0:T(2,128)(2,1)} %reshape.107), calls=%async_computation.6 | async-start | bytes 98304 | tf_op jit(solution)/shard_map/all_to_all | solution.py:82
  390.2 0.9 copy-start.9
  391.0 24.5 %all-to-all-start.8 = ((f32[16,16,512]{2,1,0:T(8,128)}), f32[16,16,512]{2,1,0:T(8,128)}, u32[]{:S(2)}, u32[]{:S(2)}) async-start(f32[16,16,512]{2,1,0:T(8,128)} %broadcast_in_dim.17), calls=%async_computation.8 | async-start | bytes 1048576 | tf_op jit(solution)/shard_map/all_to_all | solution.py:20
  399.1 1.2 copy-start.10

commit v2 on v1

--- a/solution.py
+++ b/solution.py
@@ -3,7 +3,93 @@
 import jax
 import jax.numpy as jnp
 from jax import lax
+from jax.experimental import pallas as pl
+from jax.experimental.pallas import tpu as pltpu
 from jax.sharding import PartitionSpec as P
+
+SUB, LANE = 8, 128
+HI = lax.Precision.HIGHEST
+
+def over_lanes(tile, column):
+    return jnp.broadcast_to(tile[:, column:column + 1], (SUB, LANE))
+
+def over_sublanes(tile, row):
+    return jnp.broadcast_to(tile[row:row + 1, :], (SUB, LANE))
+
+def invert_block(tiles):
+    sub = lax.broadcasted_iota(jnp.int32, (SUB, LANE), 0)
+    lane = lax.broadcasted_iota(jnp.int32, (SUB, LANE), 1)
+    tiles = list(tiles)
+    done = []
+    count = len(tiles)
+    for g in range(count):
+        first = SUB * g
+        in_panel = (lane >= first) & (lane < first + SUB)
+        rows = tiles[g]
+        columns = [over_lanes(rows, first + t) for t in range(SUB)]
+        panel = jnp.where(in_panel, (lane - first == sub).astype(jnp.float32), rows)
+        scale = jnp.ones((SUB, LANE), jnp.float32)
+        inverse, coupling, pivot_rows = [], [], []
+        for t in range(SUB):
+            pivot = over_sublanes(columns[t], t)
+            inv = 1.0 / pivot
+            inverse.append(inv)
+            pivot_rows.append(over_sublanes(panel, t))
+            scale = jnp.where(sub == t, lax.rsqrt(pivot), scale)
+            factor = jnp.where(sub > t, columns[t] * inv, 0.0)
+            couple = {}
+            for u in range(t + 1, SUB):
+                couple[u] = over_sublanes(columns[u], t)
+                columns[u] = columns[u] - factor * couple[u]
+            coupling.append(couple)
+            panel = panel - factor * pivot_rows[t]
+        done.append(panel * scale)
+        for i in range(g + 1, count):
+            cols = [over_lanes(tiles[i], first + t) for t in range(SUB)]
+            row = jnp.where(in_panel, 0.0, tiles[i])
+            for t in range(SUB):
+                f = cols[t] * inverse[t]
+                for u in range(t + 1, SUB):
+                    cols[u] = cols[u] - f * coupling[t][u]
+                row = row - f * pivot_rows[t]
+            tiles[i] = row
+    return [jnp.where(lane <= sub + SUB * g, tile, 0.0) for g, tile in enumerate(done)]
+
+def mm(a, b, dims):
+    return lax.dot_general(a, b, (dims, ((), ())), precision=HI, preferred_element_type=jnp.float32)
+
+def kernel(gram_ref, out_ref, aug):
+    n = gram_ref.shape[0]
+    blocks = n // LANE
+    aug[:, :n] = gram_ref[...]
+    aug[:, n:] = jnp.zeros((n, n), jnp.float32)
+    out_ref[...] = jnp.zeros_like(out_ref)
+    def step(k, _):
+        at = pl.multiple_of(k * LANE, LANE)
+        tiles = [aug[pl.ds(at + SUB * g, SUB), pl.ds(at, LANE)] for g in range(LANE // SUB)]
+        inv = invert_block(tiles)
+        for g, t in enumerate(inv):
+            out_ref[pl.ds(at + SUB * g, SUB), pl.ds(at, LANE)] = t
+        return _
+    for k in range(blocks):
+        lo, hi = k * LANE, (k + 1) * LANE
+        step(k, 0)
+        inv = out_ref[lo:hi, lo:hi]
+        if k:
+            out_ref[lo:hi, :lo] = mm(inv, aug[lo:hi, n:n + lo], ((1,), (0,)))
+        if k + 1 < blocks:
+            right = mm(inv, aug[lo:hi, hi:n], ((1,), (0,)))
+            aug[hi:, hi:n] -= mm(right, right, ((0,), (0,)))
+            aug[hi:, n:n + hi] -= mm(right, out_ref[lo:hi, :hi], ((0,), (0,)))
+
+def inverse_factor(gram):
+    n = gram.shape[0]
+    return pl.pallas_call(
+        kernel,
+        out_shape=jax.ShapeDtypeStruct((n, n), jnp.float32),
+        scratch_shapes=[pltpu.VMEM((n, 2 * n), jnp.float32)],
+        compiler_params=pltpu.CompilerParams(vmem_limit_bytes=32 << 20),
+    )(gram)
 
 
 def lines(axis_size, stride):
@@ -47,9 +133,8 @@
 
 
 def to_basis(sketch, gram):
-    factor = jnp.linalg.cholesky(gram)
-    solved = jax.scipy.linalg.solve_triangular(factor, sketch.T, lower=True)
-    return solved.T.astype(jnp.bfloat16)
+    solved = mm(sketch, inverse_factor(gram), ((1,), (1,)))
+    return solved.astype(jnp.bfloat16)
 
 
 def per_device(trajectory, test_matrix):

time: 423 us -> 268 us (0.63); the launches traced: 417 us -> 267 us
  other arithmetic: 136 us -> 4.14 us
  local copies, waits for them, and re-layouts: 32.7 us -> 10.3 us
  Pallas kernels: 0 us -> 19.2 us
  matrix products: 23.1 us -> 10.2 us
    another operation x17 -> x0, other arithmetic: 124 us -> none  [the longest x14 83.2 us: to_basis(): factor = jnp.linalg.cholesky(gram)]
    pallas_call x0 -> x1, Pallas kernels: none -> 19.2 us  [inverse_factor(): pl.pallas_call(kernel, out_shape=jax.ShapeDtypeStruct((n, n), jnp.float32...]
    another operation x13 -> x0, matrix products: 15.2 us -> none  [the longest x7 7.96 us: to_basis(): solved = jax.scipy.linalg.solve_triangular(factor, sketch.T, lower=True)]
    another operation x17 -> x0, local copies, waits for them, and re-layouts: 14.7 us -> none
  transfers between devices with their start and end apart: 6 -> 6, of which waited for: 5 -> 6; matrix products, arithmetic and copies ran while one was open for 2% -> 1% of each run, Pallas kernels for 0% -> 0%
where the time goes in v2:
time: 268 us; the launch traced here: 267 us
  blocking collectives  143 us (53%)
  waiting for transfers between devices  44.7 us (17%)
  starting transfers between devices  35 us (13%)
  Pallas kernels  19.2 us (7%)
  local copies, waits for them, and re-layouts  10.3 us (4%)
  matrix products  10.2 us (4%)
  other arithmetic  4.14 us (2%)
    all_to_all x3, blocking collectives, scatter_sum(): got = lax.all_to_all(blocks, axis, 0, 0, axis_index_groups=groups)  88.7 us
    all_to_all x3, blocking collectives, gather(): return lax.all_to_all(copies, axis, 0, 0, axis_index_groups=groups)  54.1 us
    pallas_call x1, Pallas kernels, inverse_factor(): pl.pallas_call(kernel, out_shape=jax.ShapeDtypeStruct((n, n), jnp.float32...  19.2 us
    ppermute x3, starting transfers between devices, swap_cores(): return lax.ppermute(block, 'feat', [(i, i ^ 1) for i in range(count)])  17.9 us
    all_to_all x1, waiting for transfers between devices, gather(): return lax.all_to_all(copies, axis, 0, 0, axis_index_groups=groups)  16.3 us
    all_to_all x1, waiting for transfers between devices, scatter_sum(): got = lax.all_to_all(blocks, axis, 0, 0, axis_index_groups=groups)  14.3 us
    all_to_all x1, waiting for transfers between devices, per_device(): swapped = lax.all_to_all(by_rows, 'frame', 0, 0)  8.65 us
    all_to_all x1, starting transfers between devices, gather(): return lax.all_to_all(copies, axis, 0, 0, axis_index_groups=groups)  6.41 us
  transfers between devices with their start and end apart: 6, of which 6 were waited for; matrix products, arithmetic and copies ran while one was open for 1% of the time, Pallas kernels for 0%

profile of v2, /device:TPU:1, one launch (start us, length us, event | category | flops | bytes accessed | tf_op | source)
XLA Modules:
  0.0 267.2 jit_solution(8328948838061610188)
XLA Ops:
  0.7 1.6 copy-done
  2.3 2.8 %fusion.11 = f32[768,512]{1,0:T(8,128)S(1)} fusion(bf16[768,1536]{1,0:T(8,128)(2,1)S(1)} %copy-done, bf16[1536,512]{1,0:T(8,128)(2,1)} %param.3), kind=kOutput, calls=%fused_computation.28 | convolution fusion | flops 1207959552 | bytes 5505024 | tf_op jit(solution)/shard_map/dot_general | solution.py:148
  5.1 1.2 copy-done.5
  6.3 0.9 dynamic-slice_bitcast_fusion
  7.2 8.8 %collective-permute-start = (f32[384,512]{1,0:T(8,128)}, f32[384,512]{1,0:T(8,128)S(1)}, u32[]{:S(2)}, u32[]{:S(2)}) collective-permute-start(f32[384,512]{1,0:T(8,128)} %dynamic-slice_bitcast_fusion), channel_id=1, source_target_pairs={{0,1},{1,0},{2,3},{3,2},{4,5},{5,4},{6,7},{7,6},{8,9},{9,8},{10,11... | collective-permute-start | bytes 2359304 | tf_op jit(solution)/shard_map/ppermute | solution.py:111
  16.0 2.1 collective-permute-done
  18.1 1.3 bitcast_add_fusion
  19.4 26.0 %all_to_all.45 = f32[8,48,512]{2,1,0:T(8,128)S(1)} all-to-all(f32[8,48,512]{2,1,0:T(8,128)S(1)} %bitcast.31), channel_id=1, replica_groups={{0,2,4,6,8,10,12,14},{1,3,5,7,9,11,13,15},{16,18,20,22,24,26,28,30},{17..., dimensions={0} | all-to-all | bytes 1572864 | tf_op jit(solution)/shard_map/all_to_all | solution.py:100
  45.5 25.9 %all_to_all.46 = f32[8,48,512]{2,1,0:T(8,128)S(1)} all-to-all(f32[8,48,512]{2,1,0:T(8,128)S(1)} %broadcast_in_dim.12), channel_id=1, replica_groups={{0,2,4,6,8,10,12,14},{1,3,5,7,9,11,13,15},{16,18,20,22,24,26,28,30},{17..., dimensions={0} | all-to-all | bytes 1572864 | tf_op jit(solution)/shard_map/all_to_all | solution.py:106
  71.4 2.5 collective-permute-start.1
  73.9 2.0 collective-permute-done.1
  75.9 1.6 broadcast_select_fusion.1
  77.5 1.1 fusion.3
  78.7 19.1 %all_to_all.47 = f32[32,1,512]{2,1,0:T(1,128)S(1)} all-to-all(f32[32,1,512]{2,1,0:T(1,128)S(1)} %copy.12), channel_id=1, replica_groups=mesh['frame'=32,'feat'=16] {'frame'}, dimensions={0} | all-to-all | bytes 131072 | tf_op jit(solution)/shard_map/all_to_all | solution.py:100
  97.9 11.9 %all_to_all.48 = f32[32,1,512]{2,1,0:T(1,128)S(1)} all-to-all(f32[32,1,512]{2,1,0:T(1,128)S(1)} %broadcast_in_dim.13), channel_id=1, replica_groups=mesh['frame'=32,'feat'=16] {'frame'}, dimensions={0} | all-to-all | bytes 131072 | tf_op jit(solution)/shard_map/all_to_all | solution.py:106
  109.9 16.3 %all_to_all.49 = f32[8,32,512]{2,1,0:T(8,128)S(1)} all-to-all(f32[8,32,512]{2,1,0:T(8,128)S(1)} %broadcast_in_dim.14), channel_id=1, replica_groups={{0,2,4,6,8,10,12,14},{1,3,5,7,9,11,13,15},{16,18,20,22,24,26,28,30},{17..., dimensions={0} | all-to-all | bytes 1048576 | tf_op jit(solution)/shard_map/all_to_all | solution.py:106
  126.1 6.7 %collective-permute-start.2 = (f32[256,512]{1,0:T(8,128)S(1)}, f32[256,512]{1,0:T(8,128)S(1)}, u32[]{:S(2)}, u32[]{:S(2)}) collective-permute-start(f32[256,512]{1,0:T(8,128)S(1)} %bitcast.33), channel_id=1, source_target_pairs={{0,1},{1,0},{2,3},{3,2},{4,5},{5,4},{6,7},{7,6},{8,9},{9,8},{10,11... | collective-permute-start | bytes 1572872 | tf_op jit(solution)/shard_map/ppermute | solution.py:111
  132.8 1.3 collective-permute-done.2
  134.4 19.2 %shard_map.49 = f32[512,512]{1,0:T(8,128)S(1)} custom-call(f32[512,512]{1,0:T(8,128)S(1)} %pad_maximum_fusion.7.gram_ref), custom_call_target="tpu_custom_call" | custom-call | tf_op jit(solution)/shard_map/pallas_call | solution.py:87
  153.6 2.7 convolution_convert_fusion.1
  156.3 0.9 copy-done.3
  157.2 2.6 fusion
  159.8 2.6 copy.13
  162.4 43.6 %all_to_all.50 = bf16[32,48,512]{2,1,0:T(8,128)(2,1)S(1)} all-to-all(bf16[32,48,512]{2,1,0:T(8,128)(2,1)} %bitcast.30), channel_id=1, replica_groups=mesh['frame'=32,'feat'=16] {'frame'}, dimensions={0} | all-to-all | bytes 3145728 | tf_op jit(solution)/shard_map/all_to_all | solution.py:100
  206.2 1.1 convolution_convert_fusion.2
  207.3 4.4 %all-to-all-start.7 = ((bf16[32,16,512]{2,1,0:T(8,128)(2,1)}), bf16[32,16,512]{2,1,0:T(8,128)(2,1)S(1)}, u32[]{:S(2)}, u32[]{:S(2)}) async-start(bf16[32,16,512]{2,1,0:T(8,128)(2,1)} %bitcast.12), calls=%async_computation.7 | async-start | bytes 1048576 | tf_op jit(solution)/shard_map/all_to_all | solution.py:100
  212.7 14.3 %all-to-all-done.7 = bf16[32,16,512]{2,1,0:T(8,128)(2,1)S(1)} async-done(((bf16[32,16,512]{2,1,0:T(8,128)(2,1)}), bf16[32,16,512]{2,1,0:T(8,128)(2,1)S(1)}, u32[]{:S(2)}, u32[]{:S(2)}) %all-to-all-start.7) | async-done | bytes 524320 | tf_op jit(solution)/shard_map/all_to_all | solution.py:100
  227.0 6.2 %all-to-all-start.6 = ((bf16[32,2,384]{2,1,0:T(2,128)(2,1)}), bf16[32,2,384]{2,1,0:T(2,128)(2,1)S(1)}, u32[]{:S(2)}, u32[]{:S(2)}) async-start(bf16[32,2,384]{2,1,0:T(2,128)(2,1)} %reshape.49), calls=%async_computation.6 | async-start | bytes 98304 | tf_op jit(solution)/shard_map/all_to_all | solution.py:167
  233.3 8.6 %all-to-all-done.6 = bf16[32,2,384]{2,1,0:T(2,128)(2,1)S(1)} async-done(((bf16[32,2,384]{2,1,0:T(2,128)(2,1)}), bf16[32,2,384]{2,1,0:T(2,128)(2,1)S(1)}, u32[]{:S(2)}, u32[]{:S(2)}) %all-to-all-start.6) | async-done | bytes 49184 | tf_op jit(solution)/shard_map/all_to_all | solution.py:167
  241.9 0.9 broadcast_in_dim.15
  242.8 6.4 %all-to-all-start.8 = ((f32[16,16,512]{2,1,0:T(8,128)}), f32[16,16,512]{2,1,0:T(8,128)S(1)}, u32[]{:S(2)}, u32[]{:S(2)}) async-start(f32[16,16,512]{2,1,0:T(8,128)} %broadcast_in_dim.15), calls=%async_computation.8 | async-start | bytes 1048576 | tf_op jit(solution)/shard_map/all_to_all | solution.py:106
  250.2 16.3 %all-to-all-done.8 = f32[16,16,512]{2,1,0:T(8,128)S(1)} async-done(((f32[16,16,512]{2,1,0:T(8,128)}), f32[16,16,512]{2,1,0:T(8,128)S(1)}, u32[]{:S(2)}, u32[]{:S(2)}) %all-to-all-start.8) | async-done | bytes 524320 | tf_op jit(solution)/shard_map/all_to_all | solution.py:106
  (28 shorter events, 3.5 us)
Async XLA Ops:
  0.6 1.7 copy-start
  5.1 1.2 copy-start.5
  7.2 10.9 %collective-permute-start = (f32[384,512]{1,0:T(8,128)}, f32[384,512]{1,0:T(8,128)S(1)}, u32[]{:S(2)}, u32[]{:S(2)}) collective-permute-start(f32[384,512]{1,0:T(8,128)} %dynamic-slice_bitcast_fusion), channel_id=1, source_target_pairs={{0,1},{1,0},{2,3},{3,2},{4,5},{5,4},{6,7},{7,6},{8,9},{9,8},{10,11... | collective-permute-start | bytes 2359304 | tf_op jit(solution)/shard_map/ppermute | solution.py:111
  71.4 2.5 copy-start.4
  71.4 4.5 %collective-permute-start.1 = (f32[384,512]{1,0:T(8,128)S(1)}, f32[384,512]{1,0:T(8,128)}, u32[]{:S(2)}, u32[]{:S(2)}) collective-permute-start(f32[384,512]{1,0:T(8,128)S(1)} %bitcast.32), channel_id=1, source_target_pairs={{0,1},{1,0},{2,3},{3,2},{4,5},{5,4},{6,7},{7,6},{8,9},{9,8},{10,11... | collective-permute-start | bytes 2359304 | tf_op jit(solution)/shard_map/ppermute | solution.py:111
  77.5 1.1 copy-start.1
  126.1 8.0 %collective-permute-start.2 = (f32[256,512]{1,0:T(8,128)S(1)}, f32[256,512]{1,0:T(8,128)S(1)}, u32[]{:S(2)}, u32[]{:S(2)}) collective-permute-start(f32[256,512]{1,0:T(8,128)S(1)} %bitcast.33), channel_id=1, source_target_pairs={{0,1},{1,0},{2,3},{3,2},{4,5},{5,4},{6,7},{7,6},{8,9},{9,8},{10,11... | collective-permute-start | bytes 1572872 | tf_op jit(solution)/shard_map/ppermute | solution.py:111
  134.4 19.3 %copy-start.2 = (f32[384,512]{1,0:T(8,128)S(1)}, f32[384,512]{1,0:T(8,128)}, u32[]{:S(2)}) copy-start(f32[384,512]{1,0:T(8,128)} %copy-done.1) | copy-start | bytes 2359300
  156.3 0.9 copy-start.3
  207.3 19.7 %all-to-all-start.7 = ((bf16[32,16,512]{2,1,0:T(8,128)(2,1)}), bf16[32,16,512]{2,1,0:T(8,128)(2,1)S(1)}, u32[]{:S(2)}, u32[]{:S(2)}) async-start(bf16[32,16,512]{2,1,0:T(8,128)(2,1)} %bitcast.12), calls=%async_computation.7 | async-start | bytes 1048576 | tf_op jit(solution)/shard_map/all_to_all | solution.py:100
  227.0 15.0 %all-to-all-start.6 = ((bf16[32,2,384]{2,1,0:T(2,128)(2,1)}), bf16[32,2,384]{2,1,0:T(2,128)(2,1)S(1)}, u32[]{:S(2)}, u32[]{:S(2)}) async-start(bf16[32,2,384]{2,1,0:T(2,128)(2,1)} %reshape.49), calls=%async_computation.6 | async-start | bytes 98304 | tf_op jit(solution)/shard_map/all_to_all | solution.py:167
  242.8 23.8 %all-to-all-start.8 = ((f32[16,16,512]{2,1,0:T(8,128)}), f32[16,16,512]{2,1,0:T(8,128)S(1)}, u32[]{:S(2)}, u32[]{:S(2)}) async-start(f32[16,16,512]{2,1,0:T(8,128)} %broadcast_in_dim.15), calls=%async_computation.8 | async-start | bytes 1048576 | tf_op jit(solution)/shard_map/all_to_all | solution.py:106

commit v3 on v2

--- a/solution.py
+++ b/solution.py
@@ -1,3 +1,4 @@
+import functools
 import math
 
 import jax
@@ -132,9 +133,25 @@
     return jnp.concatenate([low, high], axis=0)
 
 
-def to_basis(sketch, gram):
-    solved = mm(sketch, inverse_factor(gram), ((1,), (1,)))
-    return solved.astype(jnp.bfloat16)
+def tail_kernel(scale, summed_ref, inverse_ref, out_ref, wide):
+    mine, n = summed_ref.shape
+    wide[...] = jnp.zeros_like(wide)
+    wide[:mine, :] = summed_ref[...]
+    projected = (mm(inverse_ref[...], wide[...], ((1,), (1,))) * scale).astype(jnp.bfloat16)
+    out_ref[:, n:] = projected
+    out_ref[:, :n] = lax.dot_general(
+        projected, projected, (((1,), (1,)), ((), ())), preferred_element_type=jnp.float32
+    ).astype(jnp.bfloat16)
+
+
+def project(summed, inverse, scale):
+    n = inverse.shape[0]
+    return pl.pallas_call(
+        functools.partial(tail_kernel, scale),
+        out_shape=jax.ShapeDtypeStruct((n, n + LANE), jnp.bfloat16),
+        scratch_shapes=[pltpu.VMEM((LANE, n), jnp.float32)],
+        compiler_params=pltpu.CompilerParams(vmem_limit_bytes=32 << 20),
+    )(summed, inverse)
 
 
 def per_device(trajectory, test_matrix):
@@ -146,34 +163,42 @@
     rank = test_matrix.shape[1]
 
     partial_sketch = jnp.dot(trajectory, test_matrix, preferred_element_type=jnp.float32)
+    by_feature = lax.optimization_barrier(trajectory.T)
     sketch = feat_gather(feat_scatter_sum(partial_sketch))
 
     width = rank // feat_count
     place = lax.axis_index("feat") % 2 * (feat_count // 2) + lax.axis_index("feat") // 2
     columns = lax.dynamic_slice_in_dim(sketch, place * width, width, axis=1)
     gram_rows = jnp.dot(columns.T, sketch, precision=lax.Precision.HIGHEST) / frames_all
+
+    high = sketch.astype(jnp.bfloat16)
+    low = (sketch - high.astype(jnp.float32)).astype(jnp.bfloat16)
+    partial = jnp.dot(by_feature, high, preferred_element_type=jnp.float32) + jnp.dot(
+        by_feature, low, preferred_element_type=jnp.float32
+    )
+    x_count = 4
+    z_count = frame_count // x_count
+    x_groups = [list(range(s, s + x_count)) for s in range(0, frame_count, x_count)]
+    some = lax.psum_scatter(
+        partial, "frame", scatter_dimension=0, axis_index_groups=x_groups, tiled=True
+    )
+    summed = lax.psum_scatter(
+        some, "frame", scatter_dimension=0, axis_index_groups=lines(frame_count, x_count), tiled=True
+    )
+
     gram_mine = scatter_sum(gram_rows.reshape(frame_count, -1, rank), "frame")
     gram_rows = gather(gram_mine, "frame", frame_count).reshape(width, rank)
-    gram = feat_gather(gram_rows)
-
-    orthobasis = to_basis(sketch, gram)
-    partial = lax.dot_general(
-        trajectory, orthobasis, (((0,), (0,)), ((), ())), preferred_element_type=jnp.float32
-    )
-    summed = scatter_sum(partial.astype(jnp.bfloat16).reshape(frame_count, -1, rank), "frame")
-    features_mine = (summed / math.sqrt(frames_all)).astype(jnp.bfloat16)
-
-    by_rows = features_mine.T.reshape(frame_count, rank // frame_count, -1)
-    swapped = lax.all_to_all(by_rows, "frame", 0, 0)
-    projected = swapped.transpose(1, 0, 2).reshape(rank // frame_count, local_feats)
-
-    partial_gram = lax.dot_general(
-        features_mine, features_mine, (((0,), (0,)), ((), ())), preferred_element_type=jnp.float32
-    )
-    gram_mine = scatter_sum(
-        partial_gram.astype(jnp.bfloat16).reshape(frame_count, -1, rank), "frame"
-    )
-    small_gram = jnp.sum(gather(gram_mine, "feat", feat_count), axis=0) / features_all
+    inverse = inverse_factor(feat_gather(gram_rows))
+
+    orthobasis = mm(sketch, inverse, ((1,), (1,))).astype(jnp.bfloat16)
+    parts = project(summed, inverse, 1.0 / math.sqrt(frames_all))
+    got = lax.all_to_all(parts.reshape(frame_count, -1, rank + LANE), "frame", 0, 0)
+    gram_mine = jnp.sum(got[:, :, :rank].astype(jnp.float32), axis=0).astype(jnp.bfloat16)
+    small_gram = jnp.sum(gather(gram_mine, "feat", feat_count).astype(jnp.float32), axis=0) / features_all
+
+    columns = got[:, :, rank : rank + local_feats // frame_count]
+    columns = columns.reshape(z_count, x_count, rank // frame_count, -1)
+    projected = columns.transpose(2, 1, 0, 3).reshape(rank // frame_count, local_feats)
     return (orthobasis, projected, small_gram)
 
 

time: 268 us -> 229 us (0.85)
  blocking collectives: 143 us -> 103 us
  waiting for transfers between devices: 44.7 us -> 27 us
  between operations: 0.92 us -> 14.3 us
  matrix products: 10.2 us -> 14.6 us
    all_to_all x3 -> x2, blocking collectives: 88.7 us -> 45.1 us  [scatter_sum(): got = lax.all_to_all(blocks, axis, 0, 0, axis_index_groups=groups)]
    all_to_all x2 -> x0, waiting for transfers between devices: 22.9 us -> none  [the longest x1 14.3 us: scatter_sum(): got = lax.all_to_all(blocks, axis, 0, 0, axis_index_groups=groups)]
    all_to_all x0 -> x1, blocking collectives: none -> 20.4 us  [per_device(): lax.all_to_all(parts.reshape(frame_count, -1, rank + LANE), 'frame', 0, 0)]
    all_to_all x3 -> x2, blocking collectives: 54.1 us -> 37.8 us  [gather(): return lax.all_to_all(copies, axis, 0, 0, axis_index_groups=groups)]
    all_to_all x1 -> x2, starting transfers between devices: 6.41 us -> 18.2 us  [gather(): return lax.all_to_all(copies, axis, 0, 0, axis_index_groups=groups)]
    all_to_all x2 -> x0, starting transfers between devices: 10.6 us -> none  [the longest x1 6.21 us: per_device(): swapped = lax.all_to_all(by_rows, 'frame', 0, 0)]
    reduce_scatter x0 -> x2, waiting for transfers between devices: none -> 5.24 us  [the longest x1 3.86 us: per_device(): lax.psum_scatter(partial, 'frame', scatter_dimension=0, axis_index_groups...]
    convert_element_type x2 -> x0, local copies, waits for them, and re-layouts: 2.72 us -> none  [the longest x1 2.6 us: per_device(): partial.astype(jnp.bfloat16).reshape(frame_count, -1, rank)]
  transfers between devices with their start and end apart: 6 -> 7, of which waited for: 6 -> 7; matrix products, arithmetic and copies ran while one was open for 1% -> 4% of each run, Pallas kernels for 0% -> 8%
where the time goes in v3:
time: 229 us; the launch traced here: 228 us
  blocking collectives  103 us (45%)
  starting transfers between devices  35.7 us (16%)
  waiting for transfers between devices  27 us (12%)
  Pallas kernels  20.7 us (9%)
  matrix products  14.6 us (6%)
  between operations  14.3 us (6%)
  local copies, waits for them, and re-layouts  8.13 us (4%)
  other arithmetic  4.85 us (2%)
    all_to_all x2, blocking collectives, scatter_sum(): got = lax.all_to_all(blocks, axis, 0, 0, axis_index_groups=groups)  45.1 us
    all_to_all x2, blocking collectives, gather(): return lax.all_to_all(copies, axis, 0, 0, axis_index_groups=groups)  37.8 us
    all_to_all x1, blocking collectives, per_device(): lax.all_to_all(parts.reshape(frame_count, -1, rank + LANE), 'frame', 0, 0)  20.4 us
    pallas_call x1, Pallas kernels, inverse_factor(): pl.pallas_call(kernel, out_shape=jax.ShapeDtypeStruct((n, n), jnp.float32...  19.2 us
    all_to_all x2, starting transfers between devices, gather(): return lax.all_to_all(copies, axis, 0, 0, axis_index_groups=groups)  18.2 us
    ppermute x3, starting transfers between devices, swap_cores(): return lax.ppermute(block, 'feat', [(i, i ^ 1) for i in range(count)])  17.4 us
    all_to_all x2, waiting for transfers between devices, gather(): return lax.all_to_all(copies, axis, 0, 0, axis_index_groups=groups)  16.3 us
    ppermute x3, waiting for transfers between devices, swap_cores(): return lax.ppermute(block, 'feat', [(i, i ^ 1) for i in range(count)])  5.43 us
  transfers between devices with their start and end apart: 7, of which 7 were waited for; matrix products, arithmetic and copies ran while one was open for 4% of the time, Pallas kernels for 8%

profile of v3, /device:TPU:1, one launch (start us, length us, event | category | flops | bytes accessed | tf_op | source)
XLA Modules:
  0.0 228.5 jit_solution(14711915161541391604)
XLA Ops:
  7.2 1.6 copy-done
  8.8 2.8 %fusion.13 = f32[768,512]{1,0:T(8,128)S(1)} fusion(bf16[768,1536]{1,0:T(8,128)(2,1)S(1)} %copy-done, bf16[1536,512]{1,0:T(8,128)(2,1)} %param.3), kind=kOutput, calls=%fused_computation.29 | convolution fusion | flops 1207959552 | bytes 5505024 | tf_op jit(solution)/shard_map/dot_general | solution.py:165
  11.6 1.1 copy-done.6
  12.8 0.9 dynamic-slice_bitcast_fusion
  13.7 8.8 %collective-permute-start = (f32[384,512]{1,0:T(8,128)}, f32[384,512]{1,0:T(8,128)S(1)}, u32[]{:S(2)}, u32[]{:S(2)}) collective-permute-start(f32[384,512]{1,0:T(8,128)} %dynamic-slice_bitcast_fusion), channel_id=1, source_target_pairs={{0,1},{1,0},{2,3},{3,2},{4,5},{5,4},{6,7},{7,6},{8,9},{9,8},{10,11... | collective-permute-start | bytes 2359304 | tf_op jit(solution)/shard_map/ppermute | solution.py:112
  22.5 2.1 collective-permute-done
  24.6 1.3 bitcast_add_fusion
  25.9 26.0 %all_to_all.35 = f32[8,48,512]{2,1,0:T(8,128)S(1)} all-to-all(f32[8,48,512]{2,1,0:T(8,128)S(1)} %bitcast.35), channel_id=1, replica_groups={{0,2,4,6,8,10,12,14},{1,3,5,7,9,11,13,15},{16,18,20,22,24,26,28,30},{17..., dimensions={0} | all-to-all | bytes 1572864 | tf_op jit(solution)/shard_map/all_to_all | solution.py:101
  52.0 25.9 %all_to_all.36 = f32[8,48,512]{2,1,0:T(8,128)S(1)} all-to-all(f32[8,48,512]{2,1,0:T(8,128)S(1)} %broadcast_in_dim.12), channel_id=1, replica_groups={{0,2,4,6,8,10,12,14},{1,3,5,7,9,11,13,15},{16,18,20,22,24,26,28,30},{17..., dimensions={0} | all-to-all | bytes 1572864 | tf_op jit(solution)/shard_map/all_to_all | solution.py:107
  77.9 2.5 %collective-permute-start.1 = (f32[384,512]{1,0:T(8,128)S(1)}, f32[384,512]{1,0:T(8,128)}, u32[]{:S(2)}, u32[]{:S(2)}) collective-permute-start(f32[384,512]{1,0:T(8,128)S(1)} %bitcast.36), channel_id=1, source_target_pairs={{0,1},{1,0},{2,3},{3,2},{4,5},{5,4},{6,7},{7,6},{8,9},{9,8},{10,11... | collective-permute-start | bytes 2359304 | tf_op jit(solution)/shard_map/ppermute | solution.py:112
  80.4 2.0 collective-permute-done.1
  82.4 1.6 broadcast_select_fusion.1
  84.0 1.4 fusion.2
  85.5 3.1 %fusion = f32[1536,512]{1,0:T(8,128)} fusion(f32[512,1536]{0,1:T(8,128)S(1)} %fusion.2, bf16[1536,768]{0,1:T(8,128)(2,1)S(1)} %bitcast.33, f32[384,512]{1,0:T(8,128)S(1)} %get-tuple-element.4, f32[384,512]{1,0:T(8,128)S(1)} %get-tuple-element.3), kind=kOutput, calls=%fused_computation.1 | convolution fusion | flops 1210318848 | bytes 10223616 | tf_op jit(solution)/shard_map/dot_general | solution.py:176
  88.6 2.3 %fusion.1 = f32[32,1,512]{2,0,1:T(8,128)S(1)} fusion(f32[384,512]{1,0:T(8,128)} %copy-done.3, f32[384,512]{1,0:T(8,128)S(1)} %get-tuple-element.3, s32[]{:T(128)S(6)} %select_n.59), kind=kOutput, calls=%fused_computation.8 | convolution fusion | flops 151429120 | bytes 3211268 | tf_op jit(solution)/shard_map/dot_general | solution.py:172
  91.0 19.1 %all_to_all.37 = f32[32,1,512]{2,1,0:T(1,128)S(1)} all-to-all(f32[32,1,512]{2,1,0:T(1,128)S(1)} %copy.12), channel_id=1, replica_groups=mesh['frame'=32,'feat'=16] {'frame'}, dimensions={0} | all-to-all | bytes 131072 | tf_op jit(solution)/shard_map/all_to_all | solution.py:101
  110.3 11.9 %all_to_all.38 = f32[32,1,512]{2,1,0:T(1,128)S(1)} all-to-all(f32[32,1,512]{2,1,0:T(1,128)S(1)} %broadcast_in_dim.13), channel_id=1, replica_groups=mesh['frame'=32,'feat'=16] {'frame'}, dimensions={0} | all-to-all | bytes 131072 | tf_op jit(solution)/shard_map/all_to_all | solution.py:107
  122.2 0.9 broadcast_in_dim.14
  123.0 3.5 %all-to-all-start.4 = ((f32[8,32,512]{2,1,0:T(8,128)}), f32[8,32,512]{2,1,0:T(8,128)S(1)}, u32[]{:S(2)}, u32[]{:S(2)}) async-start(f32[8,32,512]{2,1,0:T(8,128)} %broadcast_in_dim.14), calls=%async_computation.4 | async-start | bytes 1048576 | tf_op jit(solution)/shard_map/all_to_all | solution.py:107
  126.6 3.9 %reduce-scatter.3.cloned.1.call-done = f32[384,512]{1,0:T(8,128)} async-done(((f32[1536,512]{1,0:T(8,128)}), f32[384,512]{1,0:T(8,128)}) %reduce-scatter.3.cloned.1.call-update) | async-done | bytes 786448 | tf_op jit(solution)/shard_map/reduce_scatter | solution.py:182
  130.4 10.4 %all-to-all-done.4 = f32[8,32,512]{2,1,0:T(8,128)S(1)} async-done(((f32[8,32,512]{2,1,0:T(8,128)}), f32[8,32,512]{2,1,0:T(8,128)S(1)}, u32[]{:S(2)}, u32[]{:S(2)}) %all-to-all-start.4) | async-done | bytes 524320 | tf_op jit(solution)/shard_map/all_to_all | solution.py:107
  140.8 6.1 %collective-permute-start.2 = (f32[256,512]{1,0:T(8,128)S(1)}, f32[256,512]{1,0:T(8,128)S(1)}, u32[]{:S(2)}, u32[]{:S(2)}) collective-permute-start(f32[256,512]{1,0:T(8,128)S(1)} %bitcast.38), channel_id=1, source_target_pairs={{0,1},{1,0},{2,3},{3,2},{4,5},{5,4},{6,7},{7,6},{8,9},{9,8},{10,11... | collective-permute-start | bytes 1572872 | tf_op jit(solution)/shard_map/ppermute | solution.py:112
  147.0 1.3 collective-permute-done.2
  148.5 19.2 %shard_map.49.inverse_ref = f32[512,512]{1,0:T(8,128)S(1)} custom-call(f32[512,512]{1,0:T(8,128)S(1)} %pad_maximum_fusion.1.gram_ref), custom_call_target="tpu_custom_call" | custom-call | tf_op jit(solution)/shard_map/pallas_call | solution.py:88
  167.7 1.4 reduce-scatter.5.cloned.1.call-done.summed_ref
  169.1 0.9 copy-done.1
  170.0 1.4 shard_map.50
  171.5 20.4 %all_to_all.39 = bf16[32,16,640]{2,1,0:T(8,128)(2,1)S(1)} all-to-all(bf16[32,16,640]{2,1,0:T(8,128)(2,1)S(1)} %bitcast.34), channel_id=1, replica_groups=mesh['frame'=32,'feat'=16] {'frame'}, dimensions={0} | all-to-all | bytes 1310720 | tf_op jit(solution)/shard_map/all_to_all | solution.py:195
  193.5 14.7 %all-to-all-start.6 = ((bf16[16,16,512]{2,1,0:T(8,128)(2,1)}), bf16[16,16,512]{2,1,0:T(8,128)(2,1)}, u32[]{:S(2)}, u32[]{:S(2)}) async-start(bf16[16,16,512]{2,1,0:T(8,128)(2,1)} %broadcast_in_dim.15), calls=%async_computation.8 | async-start | bytes 524288 | tf_op jit(solution)/shard_map/all_to_all | solution.py:107
  208.2 4.9 %convolution_convert_fusion = bf16[768,512]{1,0:T(8,128)(2,1)} fusion(f32[512,512]{1,0:T(8,128)S(1)} %shard_map.49.inverse_ref, f32[384,512]{1,0:T(8,128)} %copy-done.3, f32[384,512]{1,0:T(8,128)} %copy-done.2), kind=kOutput, calls=%fused_computation.6 | convolution fusion | flops 2416705536 | bytes 3407872 | tf_op jit(solution)/shard_map/dot_general | solution.py:60
  214.1 6.0 %all-to-all-done.6 = bf16[16,16,512]{2,1,0:T(8,128)(2,1)} async-done(((bf16[16,16,512]{2,1,0:T(8,128)(2,1)}), bf16[16,16,512]{2,1,0:T(8,128)(2,1)}, u32[]{:S(2)}, u32[]{:S(2)}) %all-to-all-start.6) | async-done | bytes 262176 | tf_op jit(solution)/shard_map/all_to_all | solution.py:107
  220.0 1.0 convert_reduce_fusion
  (30 shorter events, 3.8 us)
Async XLA Ops:
  7.2 1.7 copy-start
  7.2 123.2 %reduce-scatter.3.cloned.1.call-start = ((), (), s32[]{:S(2)}) async-start(), calls=%async_computation.9 | async-start | bytes 3932160 | tf_op jit(solution)/shard_map/reduce_scatter | solution.py:182
  11.6 1.2 copy-start.6
  13.7 10.9 %collective-permute-start = (f32[384,512]{1,0:T(8,128)}, f32[384,512]{1,0:T(8,128)S(1)}, u32[]{:S(2)}, u32[]{:S(2)}) collective-permute-start(f32[384,512]{1,0:T(8,128)} %dynamic-slice_bitcast_fusion), channel_id=1, source_target_pairs={{0,1},{1,0},{2,3},{3,2},{4,5},{5,4},{6,7},{7,6},{8,9},{9,8},{10,11... | collective-permute-start | bytes 2359304 | tf_op jit(solution)/shard_map/ppermute | solution.py:112
  77.9 2.5 %copy-start.4 = (f32[8,48,512]{2,1,0:T(8,128)}, f32[8,48,512]{2,1,0:T(8,128)S(1)}, u32[]{:S(2)}) copy-start(f32[8,48,512]{2,1,0:T(8,128)S(1)} %all_to_all.36) | copy-start | bytes 2359300
  77.9 4.5 %collective-permute-start.1 = (f32[384,512]{1,0:T(8,128)S(1)}, f32[384,512]{1,0:T(8,128)}, u32[]{:S(2)}, u32[]{:S(2)}) collective-permute-start(f32[384,512]{1,0:T(8,128)S(1)} %bitcast.36), channel_id=1, source_target_pairs={{0,1},{1,0},{2,3},{3,2},{4,5},{5,4},{6,7},{7,6},{8,9},{9,8},{10,11... | collective-permute-start | bytes 2359304 | tf_op jit(solution)/shard_map/ppermute | solution.py:112
  84.0 1.5 copy-start.3
  84.0 4.6 %copy-start.2 = (f32[384,512]{1,0:T(8,128)}, f32[384,512]{1,0:T(8,128)S(1)}, u32[]{:S(2)}) copy-start(f32[384,512]{1,0:T(8,128)S(1)} %get-tuple-element.3) | copy-start | bytes 2359300
  123.0 17.8 %all-to-all-start.4 = ((f32[8,32,512]{2,1,0:T(8,128)}), f32[8,32,512]{2,1,0:T(8,128)S(1)}, u32[]{:S(2)}, u32[]{:S(2)}) async-start(f32[8,32,512]{2,1,0:T(8,128)} %broadcast_in_dim.14), calls=%async_computation.4 | async-start | bytes 1048576 | tf_op jit(solution)/shard_map/all_to_all | solution.py:107
  126.5 42.6 %reduce-scatter.5.cloned.1.call-start = ((), (), s32[]{:S(2)}) async-start(), calls=%async_computation.10 | async-start | bytes 884736 | tf_op jit(solution)/shard_map/reduce_scatter | solution.py:185
  140.8 7.5 %collective-permute-start.2 = (f32[256,512]{1,0:T(8,128)S(1)}, f32[256,512]{1,0:T(8,128)S(1)}, u32[]{:S(2)}, u32[]{:S(2)}) collective-permute-start(f32[256,512]{1,0:T(8,128)S(1)} %bitcast.38), channel_id=1, source_target_pairs={{0,1},{1,0},{2,3},{3,2},{4,5},{5,4},{6,7},{7,6},{8,9},{9,8},{10,11... | collective-permute-start | bytes 1572872 | tf_op jit(solution)/shard_map/ppermute | solution.py:112
  169.1 0.9 copy-start.1
  191.8 0.8 copy-start.5
  193.5 26.5 %all-to-all-start.6 = ((bf16[16,16,512]{2,1,0:T(8,128)(2,1)}), bf16[16,16,512]{2,1,0:T(8,128)(2,1)}, u32[]{:S(2)}, u32[]{:S(2)}) async-start(bf16[16,16,512]{2,1,0:T(8,128)(2,1)} %broadcast_in_dim.15), calls=%async_computation.8 | async-start | bytes 524288 | tf_op jit(solution)/shard_map/all_to_all | solution.py:107
  208.2 5.0 %slice-start = ((bf16[32,16,640]{2,1,0:T(8,128)(2,1)}), bf16[32,16,48]{2,1,0:T(8,128)(2,1)S(1)}, s32[]{:S(2)}) async-start(bf16[32,16,640]{2,1,0:T(8,128)(2,1)} %copy-done.5), calls=%async_computation.11 | async-start | bytes 262144 | tf_op jit(solution)/shard_map/slice | solution.py:199
Sparse Core Ops, SparseCore 0:
  88.7 41.6 reduce-scatter.2
  133.2 35.8 reduce-scatter.4

commit v4 on v3

--- a/solution.py
+++ b/solution.py
@@ -59,38 +59,76 @@
 def mm(a, b, dims):
     return lax.dot_general(a, b, (dims, ((), ())), precision=HI, preferred_element_type=jnp.float32)
 
-def kernel(gram_ref, out_ref, aug):
-    n = gram_ref.shape[0]
+PACKED = ((0, 0), (0, 1), (0, 2), (2, 2), (2, 3))
+
+
+def gram_kernel(core_ref, half_ref, other_ref, _, out_ref):
+    core = core_ref[0]
+
+    def block(ref, i):
+        return ref[:, pl.ds(pl.multiple_of((i + core) % 4 * LANE, LANE), LANE)]
+
+    total = jnp.zeros((LANE, len(PACKED) * LANE), jnp.float32)
+    for ref in (half_ref, other_ref):
+        parts = [block(ref, i) for i in range(4)]
+        first = mm(parts[0], jnp.concatenate(parts[:3], axis=1), ((0,), (0,)))
+        second = mm(parts[2], jnp.concatenate(parts[2:], axis=1), ((0,), (0,)))
+        total = total + jnp.concatenate([first, second], axis=1)
+    out_ref[...] = total
+
+
+def gram_blocks(core, half, other, after):
+    return pl.pallas_call(
+        gram_kernel,
+        in_specs=[pl.BlockSpec(memory_space=pltpu.SMEM)]
+        + [pl.BlockSpec(memory_space=pltpu.VMEM)] * 2
+        + [pl.BlockSpec(memory_space=pl.ANY)],
+        out_shape=jax.ShapeDtypeStruct((LANE, len(PACKED) * LANE), jnp.float32),
+        compiler_params=pltpu.CompilerParams(vmem_limit_bytes=32 << 20),
+    )(core, half, other, after)
+
+
+def factor_kernel(core_ref, mine_ref, other_ref, out_ref, aug):
+    n = out_ref.shape[0]
     blocks = n // LANE
-    aug[:, :n] = gram_ref[...]
-    aug[:, n:] = jnp.zeros((n, n), jnp.float32)
+    core = core_ref[0]
+    aug[...] = jnp.zeros_like(aug)
     out_ref[...] = jnp.zeros_like(out_ref)
-    def step(k, _):
-        at = pl.multiple_of(k * LANE, LANE)
-        tiles = [aug[pl.ds(at + SUB * g, SUB), pl.ds(at, LANE)] for g in range(LANE // SUB)]
-        inv = invert_block(tiles)
-        for g, t in enumerate(inv):
-            out_ref[pl.ds(at + SUB * g, SUB), pl.ds(at, LANE)] = t
-        return _
+    for at, (i, j) in enumerate(PACKED):
+        columns = slice(at * LANE, (at + 1) * LANE)
+        mine, other = mine_ref[:, columns], other_ref[:, columns]
+        for c in range(2):
+            value = jnp.where(core == c, mine, other)
+            row, column = (i + c) % 4, (j + c) % 4
+            if row > column:
+                row, column, value = column, row, value.T
+            aug[row * LANE : (row + 1) * LANE, column * LANE : (column + 1) * LANE] = value
     for k in range(blocks):
         lo, hi = k * LANE, (k + 1) * LANE
-        step(k, 0)
+        tiles = [aug[lo + SUB * g : lo + SUB * (g + 1), lo:hi] for g in range(LANE // SUB)]
+        for g, tile in enumerate(invert_block(tiles)):
+            out_ref[lo + SUB * g : lo + SUB * (g + 1), lo:hi] = tile
         inv = out_ref[lo:hi, lo:hi]
         if k:
-            out_ref[lo:hi, :lo] = mm(inv, aug[lo:hi, n:n + lo], ((1,), (0,)))
+            out_ref[lo:hi, :lo] = mm(inv, aug[lo:hi, n : n + lo], ((1,), (0,)))
         if k + 1 < blocks:
             right = mm(inv, aug[lo:hi, hi:n], ((1,), (0,)))
             aug[hi:, hi:n] -= mm(right, right, ((0,), (0,)))
-            aug[hi:, n:n + hi] -= mm(right, out_ref[lo:hi, :hi], ((0,), (0,)))
-
-def inverse_factor(gram):
-    n = gram.shape[0]
+            aug[hi:, n : n + hi] -= mm(right, out_ref[lo:hi, :hi], ((0,), (0,)))
+
+
+def inverse_factor(core, mine, other):
+    n = 4 * LANE
     return pl.pallas_call(
-        kernel,
+        factor_kernel,
+        in_specs=[pl.BlockSpec(memory_space=pltpu.SMEM)] + [pl.BlockSpec(memory_space=pltpu.VMEM)] * 2,
         out_shape=jax.ShapeDtypeStruct((n, n), jnp.float32),
         scratch_shapes=[pltpu.VMEM((n, 2 * n), jnp.float32)],
         compiler_params=pltpu.CompilerParams(vmem_limit_bytes=32 << 20),
-    )(gram)
+        cost_estimate=pl.CostEstimate(
+            flops=20_000_000_000, bytes_accessed=8 * n * n, transcendentals=n
+        ),
+    )(core, mine, other)
 
 
 def lines(axis_size, stride):
@@ -125,12 +163,8 @@
 
 def feat_gather(block):
     count = lax.axis_size("feat")
-    core = lax.axis_index("feat") % 2
     half = gather(block, "feat", count // 2, lines(count, 2)).reshape(-1, block.shape[1])
-    other = swap_cores(half)
-    low = jnp.where(core == 0, half, other)
-    high = jnp.where(core == 0, other, half)
-    return jnp.concatenate([low, high], axis=0)
+    return half, swap_cores(half)
 
 
 def tail_kernel(scale, summed_ref, inverse_ref, out_ref, wide):
@@ -163,18 +197,17 @@
     rank = test_matrix.shape[1]
 
     partial_sketch = jnp.dot(trajectory, test_matrix, preferred_element_type=jnp.float32)
-    by_feature = lax.optimization_barrier(trajectory.T)
-    sketch = feat_gather(feat_scatter_sum(partial_sketch))
-
-    width = rank // feat_count
-    place = lax.axis_index("feat") % 2 * (feat_count // 2) + lax.axis_index("feat") // 2
-    columns = lax.dynamic_slice_in_dim(sketch, place * width, width, axis=1)
-    gram_rows = jnp.dot(columns.T, sketch, precision=lax.Precision.HIGHEST) / frames_all
+    half, other = feat_gather(feat_scatter_sum(partial_sketch))
+    core = lax.axis_index("feat") % 2
+    core_word = core.astype(jnp.int32).reshape(1)
+    sketch = jnp.concatenate(
+        [jnp.where(core == 0, half, other), jnp.where(core == 0, other, half)], axis=0
+    )
 
     high = sketch.astype(jnp.bfloat16)
     low = (sketch - high.astype(jnp.float32)).astype(jnp.bfloat16)
-    partial = jnp.dot(by_feature, high, preferred_element_type=jnp.float32) + jnp.dot(
-        by_feature, low, preferred_element_type=jnp.float32
+    partial = jnp.dot(trajectory.T, high, preferred_element_type=jnp.float32) + jnp.dot(
+        trajectory.T, low, preferred_element_type=jnp.float32
     )
     x_count = 4
     z_count = frame_count // x_count
@@ -182,13 +215,12 @@
     some = lax.psum_scatter(
         partial, "frame", scatter_dimension=0, axis_index_groups=x_groups, tiled=True
     )
-    summed = lax.psum_scatter(
-        some, "frame", scatter_dimension=0, axis_index_groups=lines(frame_count, x_count), tiled=True
-    )
-
-    gram_mine = scatter_sum(gram_rows.reshape(frame_count, -1, rank), "frame")
-    gram_rows = gather(gram_mine, "frame", frame_count).reshape(width, rank)
-    inverse = inverse_factor(feat_gather(gram_rows))
+    summed = scatter_sum(some.reshape(z_count, -1, rank), "frame", lines(frame_count, x_count))
+
+    packed = gram_blocks(core_word, half, other, partial)
+    packed = scatter_sum(packed.reshape(frame_count, -1, packed.shape[1]), "frame") / frames_all
+    packed = gather(packed, "frame", frame_count).reshape(LANE, -1)
+    inverse = inverse_factor(core_word, packed, swap_cores(packed))
 
     orthobasis = mm(sketch, inverse, ((1,), (1,))).astype(jnp.bfloat16)
     parts = project(summed, inverse, 1.0 / math.sqrt(frames_all))

time: 229 us -> 225 us (0.983)
  waiting for transfers between devices: 27 us -> 11.9 us
  blocking collectives: 103 us -> 115 us
  starting transfers between devices: 35.7 us -> 31.5 us
  local copies, waits for them, and re-layouts: 8.13 us -> 11.1 us
  Pallas kernels: 20.7 us -> 23.3 us
  matrix products: 14.6 us -> 12.2 us
    all_to_all x2 -> x1, waiting for transfers between devices: 16.3 us -> 5.95 us  [gather(): return lax.all_to_all(copies, axis, 0, 0, axis_index_groups=groups)]
    all_to_all x2 -> x1, starting transfers between devices: 18.2 us -> 9.33 us  [gather(): return lax.all_to_all(copies, axis, 0, 0, axis_index_groups=groups)]
    all_to_all x0 -> x1, starting transfers between devices: none -> 5.25 us  [scatter_sum(): got = lax.all_to_all(blocks, axis, 0, 0, axis_index_groups=groups)]
    all_to_all x2, blocking collectives: 37.8 us -> 41.7 us  [gather(): return lax.all_to_all(copies, axis, 0, 0, axis_index_groups=groups)]
    all_to_all x2, blocking collectives: 45.1 us -> 49 us  [scatter_sum(): got = lax.all_to_all(blocks, axis, 0, 0, axis_index_groups=groups)]
    reduce_scatter x1, waiting for transfers between devices: 3.86 us -> 0.02 us  [per_device(): lax.psum_scatter(partial, 'frame', scatter_dimension=0, axis_index_groups...]
    unnamed x15 -> x20, local copies, waits for them, and re-layouts: 4.5 us -> 8.14 us
    all_to_all x1, blocking collectives: 20.4 us -> 23.8 us  [per_device(): lax.all_to_all(parts.reshape(frame_count, -1, rank + LANE), 'frame', 0, 0)]
  transfers between devices with their start and end apart: 7 -> 6, of which waited for: 7 -> 4; matrix products, arithmetic and copies ran while one was open for 4% -> 3% of each run, Pallas kernels for 8% -> 10%
where the time goes in v4:
time: 225 us; the launch traced here: 224 us
  blocking collectives  115 us (51%)
  starting transfers between devices  31.5 us (14%)
  Pallas kernels  23.3 us (10%)
  between operations  14.3 us (6%)
  matrix products  12.2 us (5%)
  waiting for transfers between devices  11.9 us (5%)
  local copies, waits for them, and re-layouts  11.1 us (5%)
  other arithmetic  5.66 us (3%)
    all_to_all x2, blocking collectives, scatter_sum(): got = lax.all_to_all(blocks, axis, 0, 0, axis_index_groups=groups)  49 us
    all_to_all x2, blocking collectives, gather(): return lax.all_to_all(copies, axis, 0, 0, axis_index_groups=groups)  41.7 us
    all_to_all x1, blocking collectives, per_device(): lax.all_to_all(parts.reshape(frame_count, -1, rank + LANE), 'frame', 0, 0)  23.8 us
    pallas_call x1, Pallas kernels, inverse_factor(): pl.pallas_call(factor_kernel, in_specs=[pl.BlockSpec(memory_space=pltpu.S...  19.2 us
    ppermute x3, starting transfers between devices, swap_cores(): return lax.ppermute(block, 'feat', [(i, i ^ 1) for i in range(count)])  16.8 us
    all_to_all x1, starting transfers between devices, gather(): return lax.all_to_all(copies, axis, 0, 0, axis_index_groups=groups)  9.33 us
    unnamed x20, local copies, waits for them, and re-layouts  8.14 us
    all_to_all x1, waiting for transfers between devices, gather(): return lax.all_to_all(copies, axis, 0, 0, axis_index_groups=groups)  5.95 us
  transfers between devices with their start and end apart: 6, of which 4 were waited for; matrix products, arithmetic and copies ran while one was open for 3% of the time, Pallas kernels for 10%

profile of v4, /device:TPU:1, one launch (start us, length us, event | category | flops | bytes accessed | tf_op | source)
XLA Modules:
  0.0 224.4 jit_solution(4973789624067366108)
XLA Ops:
  7.2 1.6 copy-done
  8.8 2.8 %fusion.7 = f32[768,512]{1,0:T(8,128)S(1)} fusion(bf16[768,1536]{1,0:T(8,128)(2,1)S(1)} %copy-done, bf16[1536,512]{1,0:T(8,128)(2,1)} %param.3), kind=kOutput, calls=%fused_computation.19 | convolution fusion | flops 1207959552 | bytes 5505024 | tf_op jit(solution)/shard_map/dot_general | solution.py:199
  11.6 1.1 copy-done.9
  12.8 0.9 dynamic-slice_bitcast_fusion
  13.7 8.8 %collective-permute-start = (f32[384,512]{1,0:T(8,128)}, f32[384,512]{1,0:T(8,128)S(1)}, u32[]{:S(2)}, u32[]{:S(2)}) collective-permute-start(f32[384,512]{1,0:T(8,128)} %dynamic-slice_bitcast_fusion), channel_id=1, source_target_pairs={{0,1},{1,0},{2,3},{3,2},{4,5},{5,4},{6,7},{7,6},{8,9},{9,8},{10,11... | collective-permute-start | bytes 2359304 | tf_op jit(solution)/shard_map/ppermute | solution.py:150
  22.5 2.1 collective-permute-done
  24.6 1.3 bitcast_add_fusion
  25.9 26.0 %all_to_all.35 = f32[8,48,512]{2,1,0:T(8,128)S(1)} all-to-all(f32[8,48,512]{2,1,0:T(8,128)S(1)} %bitcast.28), channel_id=1, replica_groups={{0,2,4,6,8,10,12,14},{1,3,5,7,9,11,13,15},{16,18,20,22,24,26,28,30},{17..., dimensions={0} | all-to-all | bytes 1572864 | tf_op jit(solution)/shard_map/all_to_all | solution.py:139
  52.0 25.9 %all_to_all.36 = f32[8,48,512]{2,1,0:T(8,128)S(1)} all-to-all(f32[8,48,512]{2,1,0:T(8,128)S(1)} %broadcast_in_dim.9), channel_id=1, replica_groups={{0,2,4,6,8,10,12,14},{1,3,5,7,9,11,13,15},{16,18,20,22,24,26,28,30},{17..., dimensions={0} | all-to-all | bytes 1572864 | tf_op jit(solution)/shard_map/all_to_all | solution.py:145
  77.9 2.5 %collective-permute-start.1 = (f32[384,512]{1,0:T(8,128)S(1)}, f32[384,512]{1,0:T(8,128)}, u32[]{:S(2)}, u32[]{:S(2)}) collective-permute-start(f32[384,512]{1,0:T(8,128)S(1)} %bitcast.25), channel_id=1, source_target_pairs={{0,1},{1,0},{2,3},{3,2},{4,5},{5,4},{6,7},{7,6},{8,9},{9,8},{10,11... | collective-permute-start | bytes 2359304 | tf_op jit(solution)/shard_map/ppermute | solution.py:150
  80.4 2.0 collective-permute-done.1.other_ref
  82.4 1.4 broadcast_select_fusion.1
  83.8 1.4 fusion.3
  85.3 3.1 %fusion._ = f32[1536,512]{1,0:T(8,128)} fusion(f32[512,1536]{0,1:T(8,128)S(1)} %fusion.3, bf16[768,1536]{1,0:T(8,128)(2,1)S(1)} %copy-done, f32[384,512]{1,0:T(8,128)S(1)} %get-tuple-element.4, f32[384,512]{1,0:T(8,128)S(1)} %get-tuple-element.3), kind=kOutput, calls=%fused_computation.1 | convolution fusion | flops 1210318848 | bytes 10223616 | tf_op jit(solution)/shard_map/dot_general | solution.py:209
  88.4 1.9 copy-done.1
  90.3 2.6 %shard_map.49 = f32[128,640]{1,0:T(8,128)S(1)} custom-call(s32[1]{0:T(128)} %bitcast.5.core_ref, f32[384,512]{1,0:T(8,128)S(1)} %bitcast.26, f32[384,512]{1,0:T(8,128)} %collective-permute-done.1.other_ref, f32[1536,512]{1,0:T(8,128)S(1)} %copy-done.1), custom_call_target="tpu_custom_call" | custom-call | tf_op jit(solution)/shard_map/pallas_call | solution.py:81
  93.0 23.0 %all_to_all.37 = f32[32,4,640]{2,1,0:T(4,128)S(1)} all-to-all(f32[32,4,640]{2,1,0:T(4,128)S(1)} %reshape.40), channel_id=1, replica_groups=mesh['frame'=32,'feat'=16] {'frame'}, dimensions={0} | all-to-all | bytes 655360 | tf_op jit(solution)/shard_map/all_to_all | solution.py:139
  116.2 15.8 %all_to_all.38 = f32[32,4,640]{2,1,0:T(4,128)S(1)} all-to-all(f32[32,4,640]{2,1,0:T(4,128)S(1)} %broadcast_in_dim.10), channel_id=1, replica_groups=mesh['frame'=32,'feat'=16] {'frame'}, dimensions={0} | all-to-all | bytes 655360 | tf_op jit(solution)/shard_map/all_to_all | solution.py:145
  132.1 5.6 %collective-permute-start.2 = (f32[128,640]{1,0:T(8,128)S(1)}, f32[128,640]{1,0:T(8,128)S(1)}, u32[]{:S(2)}, u32[]{:S(2)}) collective-permute-start(f32[128,640]{1,0:T(8,128)S(1)} %reshape.41.mine_ref), channel_id=1, source_target_pairs={{0,1},{1,0},{2,3},{3,2},{4,5},{5,4},{6,7},{7,6},{8,9},{9,8},{10,11... | collective-permute-start | bytes 983048 | tf_op jit(solution)/shard_map/ppermute | solution.py:150
  137.7 5.3 %all-to-all-start.4 = ((f32[8,48,512]{2,1,0:T(8,128)}), f32[8,48,512]{2,1,0:T(8,128)}, u32[]{:S(2)}, u32[]{:S(2)}) async-start(f32[8,48,512]{2,1,0:T(8,128)} %bitcast.32), calls=%async_computation.5 | async-start | bytes 1572864 | tf_op jit(solution)/shard_map/all_to_all | solution.py:139
  143.7 1.0 copy-done.3
  144.7 1.0 copy-done.5
  145.6 19.2 %shard_map.50.inverse_ref = f32[512,512]{1,0:T(8,128)S(1)} custom-call(s32[1]{0:T(128)} %bitcast.5.core_ref, f32[128,640]{1,0:T(8,128)S(1)} %copy-done.3, f32[128,640]{1,0:T(8,128)S(1)} %copy-done.5), custom_call_target="tpu_custom_call" | custom-call | flops 20000000000 | bytes 2097152 | tf_op jit(solution)/shard_map/pallas_call | solution.py:122
  164.9 1.8 all-to-all-done.4
  166.6 1.2 reduce_sum.50.summed_ref
  167.8 1.4 shard_map.51
  169.3 23.8 %all_to_all.39 = bf16[32,16,640]{2,1,0:T(8,128)(2,1)S(1)} all-to-all(bf16[32,16,640]{2,1,0:T(8,128)(2,1)S(1)} %bitcast.27), channel_id=1, replica_groups=mesh['frame'=32,'feat'=16] {'frame'}, dimensions={0} | all-to-all | bytes 1310720 | tf_op jit(solution)/shard_map/all_to_all | solution.py:227
  193.1 0.8 copy-done.8
  194.8 9.3 %all-to-all-start.6 = ((bf16[16,16,512]{2,1,0:T(8,128)(2,1)}), bf16[16,16,512]{2,1,0:T(8,128)(2,1)}, u32[]{:S(2)}, u32[]{:S(2)}) async-start(bf16[16,16,512]{2,1,0:T(8,128)(2,1)} %broadcast_in_dim.11), calls=%async_computation.7 | async-start | bytes 524288 | tf_op jit(solution)/shard_map/all_to_all | solution.py:145
  204.1 4.9 %convolution_convert_fusion = bf16[768,512]{1,0:T(8,128)(2,1)} fusion(f32[512,512]{1,0:T(8,128)S(1)} %shard_map.50.inverse_ref, f32[384,512]{1,0:T(8,128)} %copy-done.7, f32[384,512]{1,0:T(8,128)} %copy-done.6), kind=kOutput, calls=%fused_computation.4 | convolution fusion | flops 2416705536 | bytes 3407872 | tf_op jit(solution)/shard_map/dot_general | solution.py:60
  210.0 6.0 %all-to-all-done.6 = bf16[16,16,512]{2,1,0:T(8,128)(2,1)} async-done(((bf16[16,16,512]{2,1,0:T(8,128)(2,1)}), bf16[16,16,512]{2,1,0:T(8,128)(2,1)}, u32[]{:S(2)}, u32[]{:S(2)}) %all-to-all-start.6) | async-done | bytes 262176 | tf_op jit(solution)/shard_map/all_to_all | solution.py:145
  215.9 1.0 convert_reduce_fusion
  (32 shorter events, 3.6 us)
Async XLA Ops:
  7.2 1.7 copy-start
  7.2 130.5 %reduce-scatter.2.cloned.1.call-start = ((), (), s32[]{:S(2)}) async-start(), calls=%async_computation.8 | async-start | bytes 3932160 | tf_op jit(solution)/shard_map/reduce_scatter | solution.py:215
  11.6 1.2 copy-start.9
  13.7 10.9 %collective-permute-start = (f32[384,512]{1,0:T(8,128)}, f32[384,512]{1,0:T(8,128)S(1)}, u32[]{:S(2)}, u32[]{:S(2)}) collective-permute-start(f32[384,512]{1,0:T(8,128)} %dynamic-slice_bitcast_fusion), channel_id=1, source_target_pairs={{0,1},{1,0},{2,3},{3,2},{4,5},{5,4},{6,7},{7,6},{8,9},{9,8},{10,11... | collective-permute-start | bytes 2359304 | tf_op jit(solution)/shard_map/ppermute | solution.py:150
  77.9 4.5 %collective-permute-start.1 = (f32[384,512]{1,0:T(8,128)S(1)}, f32[384,512]{1,0:T(8,128)}, u32[]{:S(2)}, u32[]{:S(2)}) collective-permute-start(f32[384,512]{1,0:T(8,128)S(1)} %bitcast.25), channel_id=1, source_target_pairs={{0,1},{1,0},{2,3},{3,2},{4,5},{5,4},{6,7},{7,6},{8,9},{9,8},{10,11... | collective-permute-start | bytes 2359304 | tf_op jit(solution)/shard_map/ppermute | solution.py:150
  83.8 1.5 copy-start.6
  83.8 1.5 copy-start.7
  88.4 1.9 copy-start.1
  132.1 10.9 %copy-start.2 = (f32[128,640]{1,0:T(8,128)}, f32[128,640]{1,0:T(8,128)S(1)}, u32[]{:S(2)}) copy-start(f32[128,640]{1,0:T(8,128)S(1)} %reshape.41.mine_ref) | copy-start | bytes 983044
  132.1 10.9 %collective-permute-start.2 = (f32[128,640]{1,0:T(8,128)S(1)}, f32[128,640]{1,0:T(8,128)S(1)}, u32[]{:S(2)}, u32[]{:S(2)}) collective-permute-start(f32[128,640]{1,0:T(8,128)S(1)} %reshape.41.mine_ref), channel_id=1, source_target_pairs={{0,1},{1,0},{2,3},{3,2},{4,5},{5,4},{6,7},{7,6},{8,9},{9,8},{10,11... | collective-permute-start | bytes 983048 | tf_op jit(solution)/shard_map/ppermute | solution.py:150
  137.7 28.9 %all-to-all-start.4 = ((f32[8,48,512]{2,1,0:T(8,128)}), f32[8,48,512]{2,1,0:T(8,128)}, u32[]{:S(2)}, u32[]{:S(2)}) async-start(f32[8,48,512]{2,1,0:T(8,128)} %bitcast.32), calls=%async_computation.5 | async-start | bytes 1572864 | tf_op jit(solution)/shard_map/all_to_all | solution.py:139
  143.0 0.7 copy-start.4
  143.7 1.0 copy-start.3
  144.7 1.0 copy-start.5
  193.1 0.8 copy-start.8
  194.8 21.1 %all-to-all-start.6 = ((bf16[16,16,512]{2,1,0:T(8,128)(2,1)}), bf16[16,16,512]{2,1,0:T(8,128)(2,1)}, u32[]{:S(2)}, u32[]{:S(2)}) async-start(bf16[16,16,512]{2,1,0:T(8,128)(2,1)} %broadcast_in_dim.11), calls=%async_computation.7 | async-start | bytes 524288 | tf_op jit(solution)/shard_map/all_to_all | solution.py:145
  204.1 5.0 %slice-start = ((bf16[32,16,640]{2,1,0:T(8,128)(2,1)}), bf16[32,16,48]{2,1,0:T(8,128)(2,1)S(1)}, s32[]{:S(2)}) async-start(bf16[32,16,640]{2,1,0:T(8,128)(2,1)} %copy-done.8), calls=%async_computation.9 | async-start | bytes 262144 | tf_op jit(solution)/shard_map/slice | solution.py:231
Sparse Core Ops, SparseCore 0:
  88.5 47.1 reduce-scatter.1

commit v5 on v4

--- a/solution.py
+++ b/solution.py
@@ -62,7 +62,8 @@
 PACKED = ((0, 0), (0, 1), (0, 2), (2, 2), (2, 3))
 
 
-def gram_kernel(core_ref, half_ref, other_ref, _, out_ref):
+def gram_kernel(core_ref, half_ref, other_ref, *refs):
+    out_ref = refs[-1]
     core = core_ref[0]
 
     def block(ref, i):
@@ -82,13 +83,13 @@
         gram_kernel,
         in_specs=[pl.BlockSpec(memory_space=pltpu.SMEM)]
         + [pl.BlockSpec(memory_space=pltpu.VMEM)] * 2
-        + [pl.BlockSpec(memory_space=pl.ANY)],
+        + [pl.BlockSpec(memory_space=pl.ANY)] * len(after),
         out_shape=jax.ShapeDtypeStruct((LANE, len(PACKED) * LANE), jnp.float32),
         compiler_params=pltpu.CompilerParams(vmem_limit_bytes=32 << 20),
-    )(core, half, other, after)
-
-
-def factor_kernel(core_ref, mine_ref, other_ref, out_ref, aug):
+    )(core, half, other, *after)
+
+
+def factor_kernel(core_ref, mine_ref, other_ref, _, out_ref, aug):
     n = out_ref.shape[0]
     blocks = n // LANE
     core = core_ref[0]
@@ -117,18 +118,20 @@
             aug[hi:, n : n + hi] -= mm(right, out_ref[lo:hi, :hi], ((0,), (0,)))
 
 
-def inverse_factor(core, mine, other):
+def inverse_factor(core, mine, other, after):
     n = 4 * LANE
     return pl.pallas_call(
         factor_kernel,
-        in_specs=[pl.BlockSpec(memory_space=pltpu.SMEM)] + [pl.BlockSpec(memory_space=pltpu.VMEM)] * 2,
+        in_specs=[pl.BlockSpec(memory_space=pltpu.SMEM)]
+        + [pl.BlockSpec(memory_space=pltpu.VMEM)] * 2
+        + [pl.BlockSpec(memory_space=pl.ANY)],
         out_shape=jax.ShapeDtypeStruct((n, n), jnp.float32),
         scratch_shapes=[pltpu.VMEM((n, 2 * n), jnp.float32)],
         compiler_params=pltpu.CompilerParams(vmem_limit_bytes=32 << 20),
         cost_estimate=pl.CostEstimate(
             flops=20_000_000_000, bytes_accessed=8 * n * n, transcendentals=n
         ),
-    )(core, mine, other)
+    )(core, mine, other, after)
 
 
 def lines(axis_size, stride):
@@ -167,25 +170,33 @@
     return half, swap_cores(half)
 
 
-def tail_kernel(scale, summed_ref, inverse_ref, out_ref, wide):
+def tail_kernel(scale, core_ref, summed_ref, inverse_ref, give_ref, keep_ref, projected_ref, wide):
     mine, n = summed_ref.shape
     wide[...] = jnp.zeros_like(wide)
     wide[:mine, :] = summed_ref[...]
     projected = (mm(inverse_ref[...], wide[...], ((1,), (1,))) * scale).astype(jnp.bfloat16)
-    out_ref[:, n:] = projected
-    out_ref[:, :n] = lax.dot_general(
-        projected, projected, (((1,), (1,)), ((), ())), preferred_element_type=jnp.float32
-    ).astype(jnp.bfloat16)
-
-
-def project(summed, inverse, scale):
+    projected_ref[...] = projected
+    for ref, half in ((give_ref, 1 - core_ref[0]), (keep_ref, core_ref[0])):
+        rows = projected_ref[pl.ds(pl.multiple_of(half * (n // 2), n // 2), n // 2), :]
+        term = lax.dot_general(
+            projected, rows, (((1,), (1,)), ((), ())), preferred_element_type=jnp.float32
+        )
+        ref[...] = term.astype(ref.dtype)
+
+
+def project(core, summed, inverse, scale):
     n = inverse.shape[0]
     return pl.pallas_call(
         functools.partial(tail_kernel, scale),
-        out_shape=jax.ShapeDtypeStruct((n, n + LANE), jnp.bfloat16),
+        in_specs=[pl.BlockSpec(memory_space=pltpu.SMEM)] + [pl.BlockSpec(memory_space=pltpu.VMEM)] * 2,
+        out_shape=[
+            jax.ShapeDtypeStruct((n, n // 2), jnp.bfloat16),
+            jax.ShapeDtypeStruct((n, n // 2), jnp.float32),
+            jax.ShapeDtypeStruct((n, LANE), jnp.bfloat16),
+        ],
         scratch_shapes=[pltpu.VMEM((LANE, n), jnp.float32)],
         compiler_params=pltpu.CompilerParams(vmem_limit_bytes=32 << 20),
-    )(summed, inverse)
+    )(core, summed, inverse)
 
 
 def per_device(trajectory, test_matrix):
@@ -206,29 +217,45 @@
 
     high = sketch.astype(jnp.bfloat16)
     low = (sketch - high.astype(jnp.float32)).astype(jnp.bfloat16)
-    partial = jnp.dot(trajectory.T, high, preferred_element_type=jnp.float32) + jnp.dot(
-        trajectory.T, low, preferred_element_type=jnp.float32
-    )
     x_count = 4
     z_count = frame_count // x_count
-    x_groups = [list(range(s, s + x_count)) for s in range(0, frame_count, x_count)]
-    some = lax.psum_scatter(
-        partial, "frame", scatter_dimension=0, axis_index_groups=x_groups, tiled=True
-    )
+    x = lax.axis_index("frame") % x_count
+
+    def product(piece):
+        size = local_feats // x_count
+        columns = lax.dynamic_slice_in_dim(trajectory, piece * size, size, axis=1)
+        return jnp.dot(columns.T, high, preferred_element_type=jnp.float32) + jnp.dot(
+            columns.T, low, preferred_element_type=jnp.float32
+        )
+
+    some, sent = [], []
+    for step in (2, 1, 3):
+        to = [(i, i // x_count * x_count + (i + step) % x_count) for i in range(frame_count)]
+        sent.append(product((x + step) % x_count))
+        some.append(lax.ppermute(sent[-1], "frame", to))
+    own = product(x)
+    some = (own + some[0]) + (some[1] + some[2])
     summed = scatter_sum(some.reshape(z_count, -1, rank), "frame", lines(frame_count, x_count))
 
-    packed = gram_blocks(core_word, half, other, partial)
+    packed = gram_blocks(core_word, half, other, sent)
     packed = scatter_sum(packed.reshape(frame_count, -1, packed.shape[1]), "frame") / frames_all
     packed = gather(packed, "frame", frame_count).reshape(LANE, -1)
-    inverse = inverse_factor(core_word, packed, swap_cores(packed))
+    inverse = inverse_factor(core_word, packed, swap_cores(packed), some)
 
     orthobasis = mm(sketch, inverse, ((1,), (1,))).astype(jnp.bfloat16)
-    parts = project(summed, inverse, 1.0 / math.sqrt(frames_all))
-    got = lax.all_to_all(parts.reshape(frame_count, -1, rank + LANE), "frame", 0, 0)
-    gram_mine = jnp.sum(got[:, :, :rank].astype(jnp.float32), axis=0).astype(jnp.bfloat16)
-    small_gram = jnp.sum(gather(gram_mine, "feat", feat_count).astype(jnp.float32), axis=0) / features_all
-
-    columns = got[:, :, rank : rank + local_feats // frame_count]
+    give, keep, columns = project(core_word, summed, inverse, 1.0 / math.sqrt(frames_all))
+    term = (keep + swap_cores(give).astype(jnp.float32)).astype(jnp.bfloat16)
+    parts = jnp.concatenate([term, columns], axis=1).reshape(frame_count, -1, rank // 2 + LANE)
+    got = lax.all_to_all(parts, "frame", 0, 0)
+    term = jnp.sum(got[:, :, : rank // 2].astype(jnp.float32), axis=0).astype(jnp.bfloat16)
+    terms = gather(term, "feat", feat_count // 2, lines(feat_count, 2))
+    mine = jnp.sum(terms.astype(jnp.float32), axis=0) / features_all
+    theirs = swap_cores(mine)
+    small_gram = jnp.concatenate(
+        [jnp.where(core == 0, mine, theirs), jnp.where(core == 0, theirs, mine)], axis=1
+    )
+
+    columns = got[:, :, rank // 2 : rank // 2 + local_feats // frame_count]
     columns = columns.reshape(z_count, x_count, rank // frame_count, -1)
     projected = columns.transpose(2, 1, 0, 3).reshape(rank // frame_count, local_feats)
     return (orthobasis, projected, small_gram)

time: 225 us -> 238 us (1.058)
  waiting for transfers between devices: 11.9 us -> 30.5 us
  starting transfers between devices: 31.5 us -> 47.2 us
  between operations: 14.3 us -> 1.13 us
  blocking collectives: 115 us -> 104 us
  matrix products: 12.2 us -> 15.3 us
    ppermute x0 -> x3, waiting for transfers between devices: none -> 22.8 us  [per_device(): some.append(lax.ppermute(sent[-1], 'frame', to))]
    ppermute x0 -> x3, starting transfers between devices: none -> 11.1 us  [per_device(): some.append(lax.ppermute(sent[-1], 'frame', to))]
    ppermute x3 -> x5, starting transfers between devices: 16.8 us -> 25.4 us  [swap_cores(): return lax.ppermute(block, 'feat', [(i, i ^ 1) for i in range(count)])]
    all_to_all x2, blocking collectives: 41.7 us -> 35.5 us  [gather(): return lax.all_to_all(copies, axis, 0, 0, axis_index_groups=groups)]
    all_to_all x1, waiting for transfers between devices: 5.95 us -> 0.01 us  [gather(): return lax.all_to_all(copies, axis, 0, 0, axis_index_groups=groups)]
    unnamed x20 -> x28, local copies, waits for them, and re-layouts: 8.14 us -> 3.55 us
    all_to_all x1, starting transfers between devices: 9.33 us -> 4.88 us  [gather(): return lax.all_to_all(copies, axis, 0, 0, axis_index_groups=groups)]
    all_to_all x1, blocking collectives: 23.8 us -> 19.7 us  [per_device(): got = lax.all_to_all(parts, 'frame', 0, 0)]
  transfers between devices with their start and end apart: 6 -> 10, of which waited for: 4 -> 6; matrix products, arithmetic and copies ran while one was open for 3% -> 4% of each run, Pallas kernels for 10% -> 9%
where the time goes in v5:
time: 238 us; the launch traced here: 237 us
  blocking collectives  104 us (44%)
  starting transfers between devices  47.2 us (20%)
  waiting for transfers between devices  30.5 us (13%)
  Pallas kernels  24.4 us (10%)
  matrix products  15.3 us (6%)
  local copies, waits for them, and re-layouts  9.3 us (4%)
  other arithmetic  4.93 us (2%)
    all_to_all x2, blocking collectives, scatter_sum(): got = lax.all_to_all(blocks, axis, 0, 0, axis_index_groups=groups)  49.2 us
    all_to_all x2, blocking collectives, gather(): return lax.all_to_all(copies, axis, 0, 0, axis_index_groups=groups)  35.5 us
    ppermute x5, starting transfers between devices, swap_cores(): return lax.ppermute(block, 'feat', [(i, i ^ 1) for i in range(count)])  25.4 us
    ppermute x3, waiting for transfers between devices, per_device(): some.append(lax.ppermute(sent[-1], 'frame', to))  22.8 us
    pallas_call x1, Pallas kernels, inverse_factor(): pl.pallas_call(factor_kernel, in_specs=[pl.BlockSpec(memory_space=pltpu.S...  20.2 us
    all_to_all x1, blocking collectives, per_device(): got = lax.all_to_all(parts, 'frame', 0, 0)  19.7 us
    ppermute x3, starting transfers between devices, per_device(): some.append(lax.ppermute(sent[-1], 'frame', to))  11.1 us
    all_to_all x1, starting transfers between devices, scatter_sum(): got = lax.all_to_all(blocks, axis, 0, 0, axis_index_groups=groups)  5.81 us
  transfers between devices with their start and end apart: 10, of which 6 were waited for; matrix products, arithmetic and copies ran while one was open for 4% of the time, Pallas kernels for 9%

profile of v5, /device:TPU:1, one launch (start us, length us, event | category | flops | bytes accessed | tf_op | source)
XLA Modules:
  0.0 237.1 jit_solution(8875652542650123076)
XLA Ops:
  0.7 1.6 copy-done
  2.3 4.0 %fusion.28 = f32[768,512]{1,0:T(8,128)} fusion(bf16[768,1536]{1,0:T(8,128)(2,1)S(1)} %copy-done, bf16[1536,512]{1,0:T(8,128)(2,1)} %param.3), kind=kOutput, calls=%fused_computation.45 | convolution fusion | flops 1207959552 | bytes 5505024 | tf_op jit(solution)/shard_map/dot_general | solution.py:210
  6.3 2.1 dynamic-slice_bitcast_fusion
  8.3 8.8 %collective-permute-start = (f32[384,512]{1,0:T(8,128)}, f32[384,512]{1,0:T(8,128)S(1)}, u32[]{:S(2)}, u32[]{:S(2)}) collective-permute-start(f32[384,512]{1,0:T(8,128)} %dynamic-slice_bitcast_fusion), channel_id=1, source_target_pairs={{0,1},{1,0},{2,3},{3,2},{4,5},{5,4},{6,7},{7,6},{8,9},{9,8},{10,11... | collective-permute-start | bytes 2359304 | tf_op jit(solution)/shard_map/ppermute | solution.py:153
  17.1 2.1 collective-permute-done
  19.2 1.3 bitcast_add_fusion
  20.5 26.0 %all_to_all.35 = f32[8,48,512]{2,1,0:T(8,128)S(1)} all-to-all(f32[8,48,512]{2,1,0:T(8,128)S(1)} %bitcast.27), channel_id=1, replica_groups={{0,2,4,6,8,10,12,14},{1,3,5,7,9,11,13,15},{16,18,20,22,24,26,28,30},{17..., dimensions={0} | all-to-all | bytes 1572864 | tf_op jit(solution)/shard_map/all_to_all | solution.py:142
  46.6 25.9 %all_to_all.36 = f32[8,48,512]{2,1,0:T(8,128)S(1)} all-to-all(f32[8,48,512]{2,1,0:T(8,128)S(1)} %broadcast_in_dim.9), channel_id=1, replica_groups={{0,2,4,6,8,10,12,14},{1,3,5,7,9,11,13,15},{16,18,20,22,24,26,28,30},{17..., dimensions={0} | all-to-all | bytes 1572864 | tf_op jit(solution)/shard_map/all_to_all | solution.py:148
  72.5 2.5 %collective-permute-start.1 = (f32[384,512]{1,0:T(8,128)S(1)}, f32[384,512]{1,0:T(8,128)}, u32[]{:S(2)}, u32[]{:S(2)}) collective-permute-start(f32[384,512]{1,0:T(8,128)S(1)} %bitcast.25), channel_id=1, source_target_pairs={{0,1},{1,0},{2,3},{3,2},{4,5},{5,4},{6,7},{7,6},{8,9},{9,8},{10,11... | collective-permute-start | bytes 2359304 | tf_op jit(solution)/shard_map/ppermute | solution.py:153
  75.1 1.9 collective-permute-done.1.other_ref
  77.0 1.3 broadcast_select_fusion.1
  81.8 2.6 %shard_map.49 = f32[128,640]{1,0:T(8,128)S(1)} custom-call(s32[1]{0:T(128)} %bitcast.5.core_ref, f32[384,512]{1,0:T(8,128)S(1)} %bitcast.26, f32[384,512]{1,0:T(8,128)} %collective-permute-done.1.other_ref, f32[384,512]{1,0:T(8,128)S(1)} %convolution_add_fusion.3.refs_0_, f32[384,512]{1,0:T(8,128)S(1)} %convolution_add_fusion.2.refs_1_, ...), custom_call_target="tpu_custom_call" | custom-call | tf_op jit(solution)/shard_map/pallas_call | solution.py:82
  86.1 23.2 %all_to_all.37 = f32[32,4,640]{2,1,0:T(4,128)S(1)} all-to-all(f32[32,4,640]{2,1,0:T(4,128)} %reshape.40), channel_id=1, replica_groups=mesh['frame'=32,'feat'=16] {'frame'}, dimensions={0} | all-to-all | bytes 655360 | tf_op jit(solution)/shard_map/all_to_all | solution.py:142
  110.2 4.9 %all-to-all-start.3 = ((f32[32,4,640]{2,1,0:T(4,128)}), f32[32,4,640]{2,1,0:T(4,128)}, u32[]{:S(2)}, u32[]{:S(2)}) async-start(f32[32,4,640]{2,1,0:T(4,128)} %broadcast_in_dim.10), calls=%async_computation.3 | async-start | bytes 655360 | tf_op jit(solution)/shard_map/all_to_all | solution.py:148
  115.1 4.6 %collective-permute-start.3 = (f32[384,512]{1,0:T(8,128)S(1)}, f32[384,512]{1,0:T(8,128)}, u32[]{:S(2)}, u32[]{:S(2)}) collective-permute-start(f32[384,512]{1,0:T(8,128)S(1)} %copy-done.2), channel_id=1, source_target_pairs={{0,32},{16,48},{32,0},{48,16},{64,96},{80,112},{96,64},{112,80},{1... | collective-permute-start | bytes 2359304 | tf_op jit(solution)/shard_map/ppermute | solution.py:235
  119.7 2.2 collective-permute-start.4
  121.9 4.3 %collective-permute-start.5 = (f32[384,512]{1,0:T(8,128)}, f32[384,512]{1,0:T(8,128)}, u32[]{:S(2)}, u32[]{:S(2)}) collective-permute-start(f32[384,512]{1,0:T(8,128)} %copy-done.4), channel_id=1, source_target_pairs={{0,48},{16,0},{32,16},{48,32},{64,112},{80,64},{96,80},{112,96},{1... | collective-permute-start | bytes 2359304 | tf_op jit(solution)/shard_map/ppermute | solution.py:235
  127.4 6.4 %collective-permute-start.2 = (f32[128,640]{1,0:T(8,128)S(1)}, f32[128,640]{1,0:T(8,128)}, u32[]{:S(2)}, u32[]{:S(2)}) collective-permute-start(f32[128,640]{1,0:T(8,128)S(1)} %reshape.41.mine_ref), channel_id=1, source_target_pairs={{0,1},{1,0},{2,3},{3,2},{4,5},{5,4},{6,7},{7,6},{8,9},{9,8},{10,11... | collective-permute-start | bytes 983048 | tf_op jit(solution)/shard_map/ppermute | solution.py:153
  133.8 1.6 fusion.3
  135.4 5.0 %collective-permute-done.3 = f32[384,512]{1,0:T(8,128)} collective-permute-done((f32[384,512]{1,0:T(8,128)S(1)}, f32[384,512]{1,0:T(8,128)}, u32[]{:S(2)}, u32[]{:S(2)}) %collective-permute-start.3) | collective-permute-done | bytes 786464 | tf_op jit(solution)/shard_map/ppermute | solution.py:235
  140.4 17.8 %collective-permute-done.4 = f32[384,512]{1,0:T(8,128)} collective-permute-done((f32[384,512]{1,0:T(8,128)}, f32[384,512]{1,0:T(8,128)}, u32[]{:S(2)}, u32[]{:S(2)}) %collective-permute-start.4) | collective-permute-done | bytes 786464 | tf_op jit(solution)/shard_map/ppermute | solution.py:235
  158.2 3.1 %fusion.1._ = f32[384,512]{1,0:T(8,128)} fusion(f32[384,512]{1,0:T(8,128)} %collective-permute-done.3, f32[384,512]{1,0:T(8,128)S(1)} %fusion.3, f32[384,512]{1,0:T(8,128)} %collective-permute-done.4, f32[384,512]{1,0:T(8,128)} %collective-permute-done.5, bf16[768,1536]{1,0:T(8,128)(2,1)S(1)} %copy-done, s32[]{:T(128)S(6)} %select_n.81, ...), kind=kOutput, calls=%fused_computation.5 | convolution fusion | flops 304349184 | bytes 6094852 | tf_op jit(solution)/shard_map/dot_general | solution.py:227
  161.3 5.8 %all-to-all-start.4 = ((f32[8,48,512]{2,1,0:T(8,128)}), f32[8,48,512]{2,1,0:T(8,128)}, u32[]{:S(2)}, u32[]{:S(2)}) async-start(f32[8,48,512]{2,1,0:T(8,128)} %bitcast.6), calls=%async_computation.4 | async-start | bytes 1572864 | tf_op jit(solution)/shard_map/all_to_all | solution.py:142
  168.1 20.2 %shard_map.50.inverse_ref = f32[512,512]{1,0:T(8,128)S(1)} custom-call(s32[1]{0:T(128)} %bitcast.5.core_ref, f32[128,640]{1,0:T(8,128)S(1)} %copy-done.6, f32[128,640]{1,0:T(8,128)} %collective-permute-done.2.other_ref, f32[384,512]{1,0:T(8,128)} %fusion.1._), custom_call_target="tpu_custom_call" | custom-call | flops 20000000000 | bytes 2097152 | tf_op jit(solution)/shard_map/pallas_call | solution.py:123
  188.3 2.5 %all-to-all-done.4 = f32[8,48,512]{2,1,0:T(8,128)} async-done(((f32[8,48,512]{2,1,0:T(8,128)}), f32[8,48,512]{2,1,0:T(8,128)}, u32[]{:S(2)}, u32[]{:S(2)}) %all-to-all-start.4) | async-done | bytes 786464 | tf_op jit(solution)/shard_map/all_to_all | solution.py:142
  190.8 1.2 reduce_sum.50.summed_ref
  192.0 1.5 shard_map.51
  193.5 2.4 %collective-permute-start.6 = (bf16[512,256]{1,0:T(8,128)(2,1)S(1)}, bf16[512,256]{1,0:T(8,128)(2,1)S(1)}, u32[]{:S(2)}, u32[]{:S(2)}) collective-permute-start(bf16[512,256]{1,0:T(8,128)(2,1)S(1)} %get-tuple-element.7), channel_id=1, source_target_pairs={{0,1},{1,0},{2,3},{3,2},{4,5},{5,4},{6,7},{7,6},{8,9},{9,8},{10,11... | collective-permute-start | bytes 786440 | tf_op jit(solution)/shard_map/ppermute | solution.py:153
  197.2 19.7 %all_to_all.38 = bf16[32,16,384]{2,1,0:T(8,128)(2,1)S(1)} all-to-all(bf16[32,16,384]{2,1,0:T(8,128)(2,1)S(1)} %bitcast.30), channel_id=1, replica_groups=mesh['frame'=32,'feat'=16] {'frame'}, dimensions={0} | all-to-all | bytes 786432 | tf_op jit(solution)/shard_map/all_to_all | solution.py:249
  216.9 9.6 %all_to_all.39 = bf16[8,16,256]{2,1,0:T(8,128)(2,1)S(1)} all-to-all(bf16[8,16,256]{2,1,0:T(8,128)(2,1)S(1)} %broadcast_in_dim.11), channel_id=1, replica_groups={{0,2,4,6,8,10,12,14},{1,3,5,7,9,11,13,15},{16,18,20,22,24,26,28,30},{17..., dimensions={0} | all-to-all | bytes 131072 | tf_op jit(solution)/shard_map/all_to_all | solution.py:148
  226.5 5.4 %collective-permute-start.7 = (f32[16,256]{1,0:T(8,128)S(1)}, f32[16,256]{1,0:T(8,128)S(1)}, u32[]{:S(2)}, u32[]{:S(2)}) collective-permute-start(f32[16,256]{1,0:T(8,128)S(1)} %broadcast_multiply_fusion), channel_id=1, source_target_pairs={{0,1},{1,0},{2,3},{3,2},{4,5},{5,4},{6,7},{7,6},{8,9},{9,8},{10,11... | collective-permute-start | bytes 49160 | tf_op jit(solution)/shard_map/ppermute | solution.py:153
  232.0 3.6 %convolution_convert_fusion = bf16[768,512]{1,0:T(8,128)(2,1)} fusion(f32[512,512]{1,0:T(8,128)S(1)} %shard_map.50.inverse_ref, f32[384,512]{1,0:T(8,128)S(1)} %copy-done.12, f32[384,512]{1,0:T(8,128)S(1)} %copy-done.9), kind=kOutput, calls=%fused_computation.2 | convolution fusion | flops 2416705536 | bytes 3407872 | tf_op jit(solution)/shard_map/dot_general | solution.py:60
  (57 shorter events, 10.9 us)
Async XLA Ops:
  0.6 1.7 copy-start
  8.3 10.9 %collective-permute-start = (f32[384,512]{1,0:T(8,128)}, f32[384,512]{1,0:T(8,128)S(1)}, u32[]{:S(2)}, u32[]{:S(2)}) collective-permute-start(f32[384,512]{1,0:T(8,128)} %dynamic-slice_bitcast_fusion), channel_id=1, source_target_pairs={{0,1},{1,0},{2,3},{3,2},{4,5},{5,4},{6,7},{7,6},{8,9},{9,8},{10,11... | collective-permute-start | bytes 2359304 | tf_op jit(solution)/shard_map/ppermute | solution.py:153
  72.5 4.5 %collective-permute-start.1 = (f32[384,512]{1,0:T(8,128)S(1)}, f32[384,512]{1,0:T(8,128)}, u32[]{:S(2)}, u32[]{:S(2)}) collective-permute-start(f32[384,512]{1,0:T(8,128)S(1)} %bitcast.25), channel_id=1, source_target_pairs={{0,1},{1,0},{2,3},{3,2},{4,5},{5,4},{6,7},{7,6},{8,9},{9,8},{10,11... | collective-permute-start | bytes 2359304 | tf_op jit(solution)/shard_map/ppermute | solution.py:153
  78.4 2.9 %copy-start.7 = (f32[384,512]{1,0:T(8,128)}, f32[384,512]{1,0:T(8,128)S(1)}, u32[]{:S(2)}) copy-start(f32[384,512]{1,0:T(8,128)S(1)} %get-tuple-element.9) | copy-start | bytes 2359300
  78.4 2.9 %copy-start.10 = (f32[384,512]{1,0:T(8,128)}, f32[384,512]{1,0:T(8,128)S(1)}, u32[]{:S(2)}) copy-start(f32[384,512]{1,0:T(8,128)S(1)} %get-tuple-element.10) | copy-start | bytes 2359300
  78.6 2.1 copy-start.13
  79.6 2.1 copy-start.1
  80.7 1.1 copy-start.3
  84.4 0.9 copy-start.4
  85.3 29.8 %copy-start.2 = (f32[384,512]{1,0:T(8,128)S(1)}, f32[384,512]{1,0:T(8,128)}, u32[]{:S(2)}) copy-start(f32[384,512]{1,0:T(8,128)} %copy-done.1) | copy-start | bytes 2359300
  110.2 16.0 %all-to-all-start.3 = ((f32[32,4,640]{2,1,0:T(4,128)}), f32[32,4,640]{2,1,0:T(4,128)}, u32[]{:S(2)}, u32[]{:S(2)}) async-start(f32[32,4,640]{2,1,0:T(4,128)} %broadcast_in_dim.10), calls=%async_computation.3 | async-start | bytes 655360 | tf_op jit(solution)/shard_map/all_to_all | solution.py:148
  115.1 25.2 %collective-permute-start.3 = (f32[384,512]{1,0:T(8,128)S(1)}, f32[384,512]{1,0:T(8,128)}, u32[]{:S(2)}, u32[]{:S(2)}) collective-permute-start(f32[384,512]{1,0:T(8,128)S(1)} %copy-done.2), channel_id=1, source_target_pairs={{0,32},{16,48},{32,0},{48,16},{64,96},{80,112},{96,64},{112,80},{1... | collective-permute-start | bytes 2359304 | tf_op jit(solution)/shard_map/ppermute | solution.py:235
  119.7 38.4 %collective-permute-start.4 = (f32[384,512]{1,0:T(8,128)}, f32[384,512]{1,0:T(8,128)}, u32[]{:S(2)}, u32[]{:S(2)}) collective-permute-start(f32[384,512]{1,0:T(8,128)} %copy-done.3), channel_id=1, source_target_pairs={{0,16},{16,32},{32,48},{48,0},{64,80},{80,96},{96,112},{112,64},{1... | collective-permute-start | bytes 2359304 | tf_op jit(solution)/shard_map/ppermute | solution.py:235
  121.9 36.2 %collective-permute-start.5 = (f32[384,512]{1,0:T(8,128)}, f32[384,512]{1,0:T(8,128)}, u32[]{:S(2)}, u32[]{:S(2)}) collective-permute-start(f32[384,512]{1,0:T(8,128)} %copy-done.4), channel_id=1, source_target_pairs={{0,48},{16,0},{32,16},{48,32},{64,112},{80,64},{96,80},{112,96},{1... | collective-permute-start | bytes 2359304 | tf_op jit(solution)/shard_map/ppermute | solution.py:235
  127.3 33.9 %copy-start.5 = (f32[128,640]{1,0:T(8,128)}, f32[128,640]{1,0:T(8,128)S(1)}, u32[]{:S(2)}) copy-start(f32[128,640]{1,0:T(8,128)S(1)} %reshape.41.mine_ref) | copy-start | bytes 983044
  127.3 30.8 %copy-start.8 = (f32[384,512]{1,0:T(8,128)S(1)}, f32[384,512]{1,0:T(8,128)}, u32[]{:S(2)}) copy-start(f32[384,512]{1,0:T(8,128)} %copy-done.7) | copy-start | bytes 2359300
  127.4 30.8 %copy-start.11 = (f32[384,512]{1,0:T(8,128)S(1)}, f32[384,512]{1,0:T(8,128)}, u32[]{:S(2)}) copy-start(f32[384,512]{1,0:T(8,128)} %copy-done.10) | copy-start | bytes 2359300
  127.4 39.7 %collective-permute-start.2 = (f32[128,640]{1,0:T(8,128)S(1)}, f32[128,640]{1,0:T(8,128)}, u32[]{:S(2)}, u32[]{:S(2)}) collective-permute-start(f32[128,640]{1,0:T(8,128)S(1)} %reshape.41.mine_ref), channel_id=1, source_target_pairs={{0,1},{1,0},{2,3},{3,2},{4,5},{5,4},{6,7},{7,6},{8,9},{9,8},{10,11... | collective-permute-start | bytes 983048 | tf_op jit(solution)/shard_map/ppermute | solution.py:153
  161.3 29.5 %all-to-all-start.4 = ((f32[8,48,512]{2,1,0:T(8,128)}), f32[8,48,512]{2,1,0:T(8,128)}, u32[]{:S(2)}, u32[]{:S(2)}) async-start(f32[8,48,512]{2,1,0:T(8,128)} %bitcast.6), calls=%async_computation.4 | async-start | bytes 1572864 | tf_op jit(solution)/shard_map/all_to_all | solution.py:142
  167.1 1.0 copy-start.6
  193.5 3.5 %collective-permute-start.6 = (bf16[512,256]{1,0:T(8,128)(2,1)S(1)}, bf16[512,256]{1,0:T(8,128)(2,1)S(1)}, u32[]{:S(2)}, u32[]{:S(2)}) collective-permute-start(bf16[512,256]{1,0:T(8,128)(2,1)S(1)} %get-tuple-element.7), channel_id=1, source_target_pairs={{0,1},{1,0},{2,3},{3,2},{4,5},{5,4},{6,7},{7,6},{8,9},{9,8},{10,11... | collective-permute-start | bytes 786440 | tf_op jit(solution)/shard_map/ppermute | solution.py:153
  197.1 34.9 %copy-start.9 = (f32[384,512]{1,0:T(8,128)S(1)}, f32[384,512]{1,0:T(8,128)}, u32[]{:S(2)}) copy-start(f32[384,512]{1,0:T(8,128)} %copy-done.7) | copy-start | bytes 2359300
  197.1 34.9 %copy-start.12 = (f32[384,512]{1,0:T(8,128)S(1)}, f32[384,512]{1,0:T(8,128)}, u32[]{:S(2)}) copy-start(f32[384,512]{1,0:T(8,128)} %copy-done.10) | copy-start | bytes 2359300
  226.5 9.9 %collective-permute-start.7 = (f32[16,256]{1,0:T(8,128)S(1)}, f32[16,256]{1,0:T(8,128)S(1)}, u32[]{:S(2)}, u32[]{:S(2)}) collective-permute-start(f32[16,256]{1,0:T(8,128)S(1)} %broadcast_multiply_fusion), channel_id=1, source_target_pairs={{0,1},{1,0},{2,3},{3,2},{4,5},{5,4},{6,7},{7,6},{8,9},{9,8},{10,11... | collective-permute-start | bytes 49160 | tf_op jit(solution)/shard_map/ppermute | solution.py:153
